TPU v7x, 512 devices: a whole 4x8x8 slice. The times are simulated.
512 devices in a mesh: blk: 16 (over x_lo, z), wide: 32 (over y, x_hi, core).
Axes of the slice: x: 4 (x_hi: 2, x_lo: 2; x = x_hi * 2 + x_lo), y: 8, z: 8, core: 2. Of those that a mesh axis runs over, the one named last changes fastest.
Arguments:
- q_latent: bfloat16 [4096, 1536], P(('blk', 'wide')), may hold values from -768 to 768
- kv_raw: bfloat16 [4096, 576], P(('blk', 'wide')), may hold values from -600 to 600
- query_plain_weight: bfloat16 [1536, 8192], P('blk', 'wide'), may hold values from -0.15625 to 0.15625
- query_rotary_weight: bfloat16 [1536, 4096], P('blk', 'wide'), may hold values from -0.15625 to 0.15625
- key_up_weight: bfloat16 [512, 8192], P('blk', 'wide'), may hold values from -0.25 to 0.25
- value_up_weight: bfloat16 [512, 8192], P('blk', 'wide'), may hold values from -0.59765625 to 0.59765625
- doc_starts: int32 [24], replicated, may hold values from 0 to 4095, as said below
- tile_kind: int32 [32, 32], P('blk'), may hold values from 0 to 2, as said below
Outputs:
- attended: bfloat16 [4096, 8192], P('blk', 'wide')
Inputs may be any that keep to these rules, and one draw needn't show every extreme that they name: doc_starts[0] = 0 and the starts rise strictly; a document runs to the next start, the last one to 4096; the longest has exactly 3072 tokens. tile_kind[i, j] is 1 where every token pair of query tile i and key tile j lies in one document with the key not after the query, 0 where no pair does, 2 otherwise; diagonal tiles are 2, so a token always sees itself.
All inputs are finite; a program needn't handle non-finite values.
Results may differ from a plain program's by a relative error of at most 0.012.
The roundings to bfloat16 on the way count: a program that leaves them out, or rounds other values in their place, can miss the bound.
Values may be sent and summed in bfloat16 or wider, within the bound.
No kernel may reach another device: no remote copies, remote signals or barrier semaphores. Data moves between devices by JAX's collectives and lax.ppermute only.
A program may use at most 64 MiB of HBM per device.

v0:
```python
import jax
import jax.numpy as jnp
from jax import lax
from jax.sharding import PartitionSpec as P

LATENT_WIDTH = 512
ROTARY_DIMS = 64
PLAIN_QUERY_DIMS = 128
VALUE_DIMS = 128
TILE = 128


def normalize_latent(kv_raw):
    value_matrix = kv_raw.astype(jnp.float32)
    latent_vectors = value_matrix[:, :LATENT_WIDTH]
    energy = jnp.mean(latent_vectors * latent_vectors, axis=1, keepdims=True)
    scaled_scores = latent_vectors * lax.rsqrt(energy + 1e-06)
    return jnp.concatenate([scaled_scores, value_matrix[:, LATENT_WIDTH:]], axis=1).astype(
        jnp.bfloat16
    )


def document_of(positions, doc_starts):
    return jnp.sum((doc_starts[None, :] <= positions[:, None]).astype(jnp.int32), axis=1) - 1


def body(
    q_latent,
    kv_raw,
    query_plain_weight,
    query_rotary_weight,
    key_up_weight,
    value_up_weight,
    doc_starts,
    tile_kind,
):
    kv_normed = normalize_latent(kv_raw)
    q_rows, kv_rows = (
        lax.all_gather(q_latent, "wide", axis=0, tiled=True),
        lax.all_gather(kv_normed, "wide", axis=0, tiled=True),
    )
    tokens_here = q_rows.shape[0]
    present_heads = key_up_weight.shape[1] // PLAIN_QUERY_DIMS
    nope_sum = jnp.dot(
        q_rows,
        lax.all_gather(query_plain_weight, "blk", axis=0, tiled=True),
        preferred_element_type=jnp.float32,
    )
    rope_sum = jnp.dot(
        q_rows,
        lax.all_gather(query_rotary_weight, "blk", axis=0, tiled=True),
        preferred_element_type=jnp.float32,
    )
    nope_sum, rope_sum = (nope_sum, rope_sum)
    key_expanded, value_expanded = (
        lax.all_gather(key_up_weight, "blk", axis=0, tiled=True),
        lax.all_gather(value_up_weight, "blk", axis=0, tiled=True),
    )
    q_nope = nope_sum.astype(jnp.bfloat16).reshape(tokens_here, present_heads, PLAIN_QUERY_DIMS)
    q_rope = rope_sum.astype(jnp.bfloat16).reshape(tokens_here, present_heads, ROTARY_DIMS)
    per_head_keys = key_expanded.reshape(LATENT_WIDTH, present_heads, PLAIN_QUERY_DIMS)
    q_absorbed = jnp.einsum(
        "thn,chn->thc", q_nope, per_head_keys, preferred_element_type=jnp.float32
    ).astype(jnp.bfloat16)
    query = jnp.concatenate([q_absorbed, q_rope], axis=2)
    first_row = lax.axis_index("blk") * tokens_here
    q_pos = first_row + jnp.arange(tokens_here, dtype=jnp.int32)
    q_doc = document_of(q_pos, doc_starts)
    q_tiles = tile_kind.shape[0]
    n_tiles = tile_kind.shape[1]
    scale = (PLAIN_QUERY_DIMS + ROTARY_DIMS) ** (-0.5)
    segment_slice = lax.all_gather(kv_rows, "blk", axis=0, tiled=True)
    count = segment_slice.shape[0]
    k_pos = jnp.arange(count, dtype=jnp.int32)
    k_doc = document_of(k_pos, doc_starts)
    chosen = (jnp.arange(n_tiles, dtype=jnp.int32)[:, None] == (k_pos // TILE)[None, :]).astype(
        jnp.int32
    )
    kinds = jnp.dot(tile_kind, chosen)
    kind_rows = jnp.broadcast_to(kinds[:, None, :], (q_tiles, TILE, count)).reshape(
        tokens_here, count
    )
    running = jnp.full((tokens_here, present_heads), -1e30, jnp.float32)
    same_doc = q_doc[:, None] == k_doc[None, :]
    causal = k_pos[None, :] <= q_pos[:, None]
    allowed = (kind_rows == 1) | (kind_rows == 2) & same_doc & causal
    scores = (
        jnp.einsum("thc,kc->thk", query, segment_slice, preferred_element_type=jnp.float32) * scale
    )
    scores = jnp.where(allowed[:, None, :], scores, -jnp.inf)
    highest = jnp.maximum(running, jnp.max(scores, axis=2))
    weights = jnp.exp(scores - highest[:, :, None])
    total = jnp.sum(weights, axis=2)
    product = jnp.einsum(
        "thk,kc->thc",
        weights.astype(jnp.bfloat16),
        segment_slice[:, :LATENT_WIDTH],
        preferred_element_type=jnp.float32,
    )
    accum = product
    running, total, accum = (highest, total, accum)
    latent_out = (accum / total[:, :, None]).astype(jnp.bfloat16)
    per_head_values = value_expanded.reshape(LATENT_WIDTH, present_heads, VALUE_DIMS)
    result_heads = jnp.einsum(
        "thc,chv->thv", latent_out, per_head_values, preferred_element_type=jnp.float32
    )
    return result_heads.reshape(tokens_here, present_heads * VALUE_DIMS).astype(jnp.bfloat16)


def solution(mesh):
    return jax.shard_map(
        body,
        mesh=mesh,
        in_specs=(
            P(("blk", "wide"), None),
            P(("blk", "wide"), None),
            P("blk", "wide"),
            P("blk", "wide"),
            P("blk", "wide"),
            P("blk", "wide"),
            P(),
            P("blk", None),
        ),
        out_specs=P("blk", "wide"),
        check_vma=False,
    )
```

profile of v0, /device:TPU:32, one launch (start us, length us, event | category | flops | bytes accessed | tf_op | source)
XLA Modules:
  0.0 272.7 jit_solution(10717325185270979151)
XLA Ops:
  6.5 0.0 copy-start
  6.5 0.0 all-gather.2.cloned.1.call-start
  6.5 0.8 fusion.24
  7.4 0.7 slice.15
  8.0 0.8 fusion.25
  8.8 40.2 %all_gather.25 = bf16[256,576]{1,0:T(8,128)(2,1)S(1)} all-gather(bf16[8,576]{1,0:T(8,128)(2,1)S(1)} %pad_maximum_fusion), channel_id=1, replica_groups=mesh['blk'=16,'wide'=32] {'wide'}, dimensions={0}, use_global_device_ids=true | all-gather | bytes 304128 | tf_op jit(solution)/shard_map/all_gather | solution.py:40
  49.1 0.9 copy.37
  49.9 0.0 all-gather.2.cloned.1.call-update
  50.0 41.1 %all_gather.23 = bf16[512,256]{1,0:T(8,128)(2,1)S(1)} all-gather(bf16[32,256]{1,0:T(8,128)(2,1)} %param.12), channel_id=1, replica_groups=mesh['blk'=16,'wide'=32] {'blk'}, dimensions={0}, use_global_device_ids=true | all-gather | bytes 278528 | tf_op jit(solution)/shard_map/all_gather | solution.py:56
  91.0 0.1 copy.33
  91.2 33.6 %all_gather.24 = bf16[1536,128]{1,0:T(8,128)(2,1)S(1)} all-gather(bf16[96,128]{1,0:T(8,128)(2,1)} %param.11), channel_id=1, replica_groups=mesh['blk'=16,'wide'=32] {'blk'}, dimensions={0}, use_global_device_ids=true | all-gather | bytes 417792 | tf_op jit(solution)/shard_map/all_gather | solution.py:51
  124.8 49.1 %all_gather.21 = bf16[256,1536]{1,0:T(8,128)(2,1)S(1)} all-gather(bf16[8,1536]{1,0:T(8,128)(2,1)} %param.8), channel_id=1, replica_groups=mesh['blk'=16,'wide'=32] {'wide'}, dimensions={0}, use_global_device_ids=true | all-gather | bytes 811008 | tf_op jit(solution)/shard_map/all_gather | solution.py:39
  173.9 0.4 convolution_convert_fusion.3
  174.3 0.1 copy.36
  174.4 32.3 %all_gather.27 = bf16[512,256]{1,0:T(8,128)(2,1)S(1)} all-gather(bf16[32,256]{1,0:T(8,128)(2,1)} %param.13), channel_id=1, replica_groups=mesh['blk'=16,'wide'=32] {'blk'}, dimensions={0}, use_global_device_ids=true | all-gather | bytes 278528 | tf_op jit(solution)/shard_map/all_gather | solution.py:57
  206.7 0.1 copy.40
  206.9 0.7 convert_reduce_fusion.1
  207.6 0.8 convert_reduce_fusion
  208.4 0.0 copy-done
  208.4 0.3 compare_bitcast_fusion.1
  208.8 1.6 fusion.11
  210.3 34.9 %all_gather.22 = bf16[1536,256]{1,0:T(8,128)(2,1)S(1)} all-gather(bf16[96,256]{1,0:T(8,128)(2,1)} %param.10), channel_id=1, replica_groups=mesh['blk'=16,'wide'=32] {'blk'}, dimensions={0}, use_global_device_ids=true | all-gather | bytes 835584 | tf_op jit(solution)/shard_map/all_gather | solution.py:46
  245.2 0.4 convolution_convert_fusion.2
  245.6 0.3 fusion.13
  246.0 0.0 all-gather.2.cloned.1.call-done
  246.0 6.1 %fusion = (f32[256,2]{0,1:T(2,128)S(1)}, f32[256,2,4096]{2,0,1:T(8,128)S(1)}) fusion(pred[256,4096]{1,0:T(8,128)(4,1)S(1)} %fusion.11, bf16[4096,576]{0,1:T(8,128)(2,1)} %all-gather.2.cloned.1.call-done, bf16[256,2,64]{2,0,1:T(8,128)(2,1)S(1)} %copy.36, bf16[256,2,512]{2,0,1:T(8,128)(2,1)S(1)} %fusion.13), kind=kOutput, calls=%fused_computation.2 | convolution fusion | flops 2423389696 | bytes 14747648 | tf_op jit(solution)/shard_map/thc,kc->thk/dot_general | solution.py:88
  252.1 0.0 copy-start.1
  252.1 3.2 %copy-done.1 = f32[256,2,4096]{2,0,1:T(8,128)} copy-done((f32[256,2,4096]{2,0,1:T(8,128)}, f32[256,2,4096]{2,0,1:T(8,128)S(1)}, u32[]{:S(2)}) %copy-start.1) | copy-done | bytes 8388632
  255.3 2.3 fusion.1
  257.7 7.4 %convolution_convert_fusion.1 = bf16[2,256,128]{1,2,0:T(8,128)(2,1)S(1)} fusion(bf16[512,2,128]{0,2,1:T(8,128)(2,1)S(1)} %bitcast.42, bf16[4096,576]{0,1:T(8,128)(2,1)} %all-gather.2.cloned.1.call-done, f32[256,2,4096]{2,0,1:T(8,128)} %copy-done.1, f32[256,2]{0,1:T(2,128)S(1)} %broadcast_maximum_fusion, pred[256,4096]{1,0:T(8,128)(4,1)S(1)} %fusion.11, ...), kind=kOutput, calls=%fused_computation.19 | convolution fusion | flops 2223570944 | bytes 14028800 | tf_op jit(solution)/shard_map/thc,chv->thv/dot_general | solution.py:104
  265.0 0.8 copy.41
  (7 shorter events, 0.0 us)
Async XLA Ops:
  6.5 201.9 %copy-start = (s32[2,32]{1,0:T(2,128)S(1)}, s32[2,32]{1,0:T(2,128)}, u32[]{:S(2)}) copy-start(s32[2,32]{1,0:T(2,128)} %param.15) | copy-start | bytes 772
  6.5 239.4 %all-gather.2.cloned.1.call-start = ((), (), s32[]{:S(2)}) async-start(), calls=%async_computation | async-start | bytes 5013504 | tf_op jit(solution)/shard_map/all_gather | solution.py:72
  252.1 3.2 %copy-start.1 = (f32[256,2,4096]{2,0,1:T(8,128)}, f32[256,2,4096]{2,0,1:T(8,128)S(1)}, u32[]{:S(2)}) copy-start(f32[256,2,4096]{2,0,1:T(8,128)S(1)} %get-tuple-element.8) | copy-start | bytes 25165828
Sparse Core Ops, SparseCore 0:
  50.1 103.2 all-gather.1
where the time goes:
time: 273 us
  blocking collectives  231 us (85%)
  matrix products  15 us (5%)
  between operations  13.5 us (5%)
  other arithmetic  7.05 us (3%)
  local copies, waits for them, and re-layouts  5.93 us (2%)
    all_gather x1, blocking collectives, body(): lax.all_gather(q_latent, 'wide', axis=0, tiled=True)  49.1 us
    all_gather x1, blocking collectives, body(): lax.all_gather(key_up_weight, 'blk', axis=0, tiled=True)  41.1 us
    all_gather x1, blocking collectives, body(): lax.all_gather(kv_normed, 'wide', axis=0, tiled=True)  40.2 us
    all_gather x1, blocking collectives, body(): lax.all_gather(query_plain_weight, 'blk', axis=0, tiled=True)  34.9 us
    all_gather x1, blocking collectives, body(): lax.all_gather(query_rotary_weight, 'blk', axis=0, tiled=True)  33.6 us
    all_gather x1, blocking collectives, body(): lax.all_gather(value_up_weight, 'blk', axis=0, tiled=True)  32.3 us
    dot_general x1, matrix products, body(): jnp.einsum('thc,chv->thv', latent_out, per_head_values, preferred_element...  7.39 us
    dot_general x1, matrix products, body(): jnp.einsum('thc,kc->thk', query, segment_slice, preferred_element_type=jn...  6.1 us
  transfers between devices with their start and end apart: 1, of which 0 were waited for; matrix products, arithmetic and copies ran while one was open for 2% of the time, Pallas kernels for 0%

commit v1 on v0

v1 whole, which is shorter than its diff:
```python
import jax
import jax.numpy as jnp
import numpy as np
from jax import lax
from jax.experimental import pallas as pl
from jax.experimental.pallas import tpu as pltpu
from jax.sharding import Mesh, PartitionSpec as P

LATENT_WIDTH = 512
ROTARY_DIMS = 64
PLAIN_QUERY_DIMS = 128
VALUE_DIMS = 128
TILE = 128
WIDTH = 640
KEY_STEP = 512
SCALE = (PLAIN_QUERY_DIMS + ROTARY_DIMS) ** (-0.5)
LOG2E = 1.4426950408889634
NEG = -1e30

AXES = ("xl", "z", "y2", "y1", "xh", "c")
SIZES = (2, 8, 4, 2, 2, 2)
BLK = ("xl", "z")
WIDE = ("y2", "y1", "xh", "c")


def normalize_latent(kv_raw):
    value_matrix = kv_raw.astype(jnp.float32)
    latent_vectors = value_matrix[:, :LATENT_WIDTH]
    energy = jnp.mean(latent_vectors * latent_vectors, axis=1, keepdims=True)
    scaled = latent_vectors * lax.rsqrt(energy + 1e-06)
    return jnp.concatenate([scaled, value_matrix[:, LATENT_WIDTH:]], axis=1).astype(jnp.bfloat16)


def swap(x, axis):
    return lax.ppermute(x, axis, [(0, 1), (1, 0)])


def in_order(bit, own, other, axis):
    first = jnp.where(bit == 0, own, other)
    second = jnp.where(bit == 0, other, own)
    return jnp.concatenate([first, second], axis=axis)


def attention_kernel(q_ref, *refs):
    pieces = refs[:-6]
    low_ref, high_ref, bounds_ref, vu_ref, o_ref, s_ref = refs[-6:]
    q = q_ref[...]
    rows = q.shape[0]
    groups = rows // TILE
    half = groups // 2
    chunks = []
    at = 0
    for ref in pieces:
        for start in range(0, ref.shape[0], KEY_STEP):
            chunks.append((ref, start, at))
            at += KEY_STEP
    highest = [jnp.full((TILE, 128), NEG, jnp.float32) for _ in range(groups)]
    for ref, start, at in chunks:
        keys = ref[pl.ds(start, KEY_STEP), :]
        scores = lax.dot_general(
            q, keys, (((1,), (1,)), ((), ())), preferred_element_type=jnp.float32
        )
        for tile in range(half):
            last = bounds_ref[pl.ds(tile * TILE, TILE), 0:1]
            first = bounds_ref[pl.ds(tile * TILE, TILE), 1:2]
            low = low_ref[tile : tile + 1, pl.ds(at, KEY_STEP)]
            high = high_ref[tile : tile + 1, pl.ds(at, KEY_STEP)]
            allowed = (low <= last) & (high >= first)
            for head in range(2):
                g = head * half + tile
                part = jnp.where(allowed, scores[g * TILE : (g + 1) * TILE, :], NEG)
                s_ref[pl.ds(g * TILE, TILE), pl.ds(at, KEY_STEP)] = part
                top = highest[g]
                for lane in range(0, KEY_STEP, 128):
                    top = jnp.maximum(top, part[:, lane : lane + 128])
                highest[g] = top
    factor = SCALE * LOG2E
    peak = [jnp.max(h, axis=1, keepdims=True) for h in highest]
    sums = [jnp.zeros((TILE, 128), jnp.float32) for _ in range(groups)]
    accum = jnp.zeros((rows, LATENT_WIDTH), jnp.float32)
    for ref, start, at in chunks:
        parts = []
        for g in range(groups):
            part = s_ref[pl.ds(g * TILE, TILE), pl.ds(at, KEY_STEP)]
            weights = jnp.exp2((part - peak[g]) * factor)
            total = sums[g]
            for lane in range(0, KEY_STEP, 128):
                total = total + weights[:, lane : lane + 128]
            sums[g] = total
            parts.append(weights.astype(jnp.bfloat16))
        accum = accum + jnp.dot(
            jnp.concatenate(parts, axis=0),
            ref[pl.ds(start, KEY_STEP), 0:LATENT_WIDTH],
            preferred_element_type=jnp.float32,
        )
    totals = jnp.concatenate([jnp.sum(s, axis=1, keepdims=True) for s in sums], axis=0)
    latent_out = (accum / totals).astype(jnp.bfloat16)
    tokens = rows // 2
    for head in range(2):
        cols = pl.ds(head * VALUE_DIMS, VALUE_DIMS)
        o_ref[:, cols] = jnp.dot(
            latent_out[head * tokens : (head + 1) * tokens, :],
            vu_ref[:, cols],
            preferred_element_type=jnp.float32,
        ).astype(jnp.bfloat16)


def attention(query, pieces, low, high, bounds, value_up):
    tokens = query.shape[0] // 2
    count = low.shape[1]
    vmem = pl.BlockSpec(memory_space=pltpu.VMEM)
    return pl.pallas_call(
        attention_kernel,
        out_shape=jax.ShapeDtypeStruct((tokens, 2 * VALUE_DIMS), jnp.bfloat16),
        in_specs=[vmem] * (len(pieces) + 5),
        out_specs=vmem,
        scratch_shapes=[pltpu.VMEM((2 * tokens, count), jnp.float32)],
        compiler_params=pltpu.CompilerParams(vmem_limit_bytes=48 * 1024 * 1024),
        cost_estimate=pl.CostEstimate(
            flops=2 * 2 * tokens * count * (576 + 512),
            bytes_accessed=count * WIDTH * 2,
            transcendentals=2 * tokens * count,
        ),
    )(query, *pieces, low, high, bounds, value_up)


def body(
    q_latent,
    kv_raw,
    query_plain_weight,
    query_rotary_weight,
    key_up_weight,
    value_up_weight,
    doc_starts,
    tile_kind,
):
    xl, z = lax.axis_index("xl"), lax.axis_index("z")
    y1, xh, core = lax.axis_index("y1"), lax.axis_index("xh"), lax.axis_index("c")
    bf16 = jnp.bfloat16

    q_far = swap(q_latent, "xh")
    kv = normalize_latent(kv_raw)
    kv_rows = jnp.concatenate(
        [kv[:, 0:256], kv[:, 256:512], jnp.pad(kv[:, 512:576], ((0, 0), (0, 192))), jnp.zeros((8, 256), bf16)],
        axis=0,
    )
    right = jnp.concatenate([key_up_weight, value_up_weight, kv_rows], axis=0)
    packed = jnp.concatenate([query_plain_weight, query_rotary_weight, right], axis=1)
    by_z = lax.all_gather(packed, "z")
    w_other = swap(by_z, "xl")
    kv_z = jnp.concatenate(
        [by_z[:, 64:72, 384:640], by_z[:, 72:80, 384:640], by_z[:, 80:88, 384:512]], axis=2
    ).reshape(64, WIDTH)

    both = jnp.stack([q_latent, q_far], axis=0)
    q_rows = both.reshape(2, 8, 3, 512).transpose(2, 0, 1, 3).reshape(48, 512)
    q_rows = jnp.pad(q_rows, ((0, 0), (0, WIDTH - 512)))
    slot = jnp.concatenate([kv_z, q_rows], axis=0)
    by_y = lax.all_to_all(jnp.broadcast_to(slot[None], (4,) + slot.shape), "y2", 0, 0)
    near = by_y[:, 0:64, :].reshape(256, WIDTH)
    q_near = by_y[:, 64:112, 0:512]

    next_y = swap(near, "y1")
    x2_near = swap(near, "xh")
    q_next = swap(q_near, "y1")
    pair = jnp.concatenate([near, next_y], axis=0)
    x1_pair = swap(pair, "xl")
    x3_pair = lax.ppermute(pair, ("xl", "xh"), [(0, 3), (3, 0), (1, 2), (2, 1)])
    x2_next = swap(x2_near, "y1")
    x2_pair = jnp.concatenate([x2_near, x2_next], axis=0)

    def q_block(q_near, q_next):
        both_y = in_order(y1, q_near[:, None], q_next[:, None], 1)
        parts = both_y.reshape(4, 2, 3, 2, 8, 512)
        both_x = in_order(xh, parts[:, :, :, 0:1], parts[:, :, :, 1:2], 3)
        return both_x

    q_half = q_block(q_near, q_next)
    q_half = q_half.transpose(0, 1, 3, 4, 2, 5).reshape(16, 8, 1536)
    q_core = swap(q_half, "c")
    q_all = in_order(core, q_half[:, None], q_core[:, None], 1).reshape(256, 1536)

    def halves(x):
        return x[:, :, 0:384].reshape(768, 384)

    own_cols = jnp.where(xl == 0, q_all[:, 0:768], q_all[:, 768:1536])
    other_cols = jnp.where(xl == 0, q_all[:, 768:1536], q_all[:, 0:768])
    projected = jnp.dot(own_cols, halves(by_z), preferred_element_type=jnp.float32) + jnp.dot(
        other_cols, halves(w_other), preferred_element_type=jnp.float32
    )
    projected = projected.astype(bf16)

    def latent_rows(first):
        own = by_z[:, first : first + 32, 384:640].reshape(256, 256)
        other = w_other[:, first : first + 32, 384:640].reshape(256, 256)
        return in_order(xl, own, other, 0)

    key_up, value_up = latent_rows(0), latent_rows(32)
    heads = []
    for head in range(2):
        cols = slice(head * PLAIN_QUERY_DIMS, (head + 1) * PLAIN_QUERY_DIMS)
        absorbed = lax.dot_general(
            projected[:, cols], key_up[:, cols], (((1,), (1,)), ((), ())), preferred_element_type=jnp.float32
        ).astype(bf16)
        rope = projected[:, 256 + head * ROTARY_DIMS : 256 + (head + 1) * ROTARY_DIMS]
        heads.append(jnp.concatenate([absorbed, rope, jnp.zeros((256, 64), bf16)], axis=1))
    query = jnp.concatenate(heads, axis=0)

    mine = [pair, x1_pair, x2_pair, x3_pair]
    theirs = [swap(piece, "c") for piece in mine]

    shape = (2, 4, 2, 4, 8, 8)
    at = lambda d: lax.broadcasted_iota(jnp.int32, shape, d)
    far = at(1)
    k_xl, k_xh = xl ^ (far & 1), xh ^ (far >> 1)
    k_block = k_xl * 8 + at(4)
    k_y = 2 * at(3) + (y1 ^ at(2))
    k_pos = (k_block * 256 + ((k_y * 2 + k_xh) * 2 + (core ^ at(0))) * 8 + at(5)).reshape(1, 4096)
    k_tile = k_pos // TILE
    kinds = jnp.sum(
        jnp.where(
            lax.broadcasted_iota(jnp.int32, (1, 32, 4096), 1) == k_tile[:, None, :], tile_kind[:, :, None], 0
        ),
        axis=1,
    )
    big = jnp.int32(1 << 20)
    low = jnp.where(kinds == 2, k_pos, jnp.where(kinds == 1, -1, big))
    high = jnp.where(kinds == 2, k_pos, jnp.where(kinds == 1, big, -1))
    q_pos = (xl * 8 + z) * 256 + lax.broadcasted_iota(jnp.int32, (256, 1), 0)
    q_first = jnp.max(jnp.where(doc_starts[None, :] <= q_pos, doc_starts[None, :], 0), axis=1, keepdims=True)
    bounds = jnp.concatenate([q_pos, q_first], axis=1)
    return attention(query, mine + theirs, low, high, bounds, value_up)


def solution(mesh):
    fine = Mesh(np.asarray(mesh.devices).reshape(SIZES), AXES)
    return jax.shard_map(
        body,
        mesh=fine,
        in_specs=(
            P(AXES, None),
            P(AXES, None),
            P(BLK, WIDE),
            P(BLK, WIDE),
            P(BLK, WIDE),
            P(BLK, WIDE),
            P(),
            P(BLK, None),
        ),
        out_specs=P(BLK, WIDE),
        check_vma=False,
    )
```

time: 273 us -> 125 us (0.46)
  the two profiles are of different devices: /device:TPU:32 before, /device:TPU:1 now
where the time goes in v1:
time: 125 us; the launch traced here: 124 us
  starting transfers between devices  54.5 us (44%)
  blocking collectives  27.3 us (22%)
  waiting for transfers between devices  16.7 us (13%)
  Pallas kernels  9.39 us (8%)
  local copies, waits for them, and re-layouts  9.08 us (7%)
  other arithmetic  5.45 us (4%)
    ppermute x12, starting transfers between devices, swap(): return lax.ppermute(x, axis, [(0, 1), (1, 0)])  43.9 us
    all_gather x1, blocking collectives, body(): by_z = lax.all_gather(packed, 'z')  27.3 us
    all_to_all x1, waiting for transfers between devices, body(): lax.all_to_all(jnp.broadcast_to(slot[None], (4,) + slot.shape), 'y2', 0, 0)  9.39 us
    pallas_call x1, Pallas kernels, attention(): pl.pallas_call(attention_kernel, out_shape=jax.ShapeDtypeStruct((tokens,...  9.39 us
    ppermute x12, waiting for transfers between devices, swap(): return lax.ppermute(x, axis, [(0, 1), (1, 0)])  7.28 us
    all_to_all x1, starting transfers between devices, body(): lax.all_to_all(jnp.broadcast_to(slot[None], (4,) + slot.shape), 'y2', 0, 0)  6.95 us
    unnamed x18, local copies, waits for them, and re-layouts  5.21 us
    ppermute x1, starting transfers between devices, body(): x3_pair = lax.ppermute(pair, ('xl', 'xh'), [(0, 3), (3, 0), (1, 2), (2, 1)])  3.72 us
  transfers between devices with their start and end apart: 14, of which 3 were waited for; matrix products, arithmetic and copies ran while one was open for 10% of the time, Pallas kernels for 0%

profile of v1, /device:TPU:1, one launch (start us, length us, event | category | flops | bytes accessed | tf_op | source)
XLA Modules:
  0.0 124.2 jit_solution(13182808237136405699)
XLA Ops:
  0.0 5.5 %collective-permute-start = (bf16[8,1536]{1,0:T(8,128)(2,1)}, bf16[8,1536]{1,0:T(8,128)(2,1)S(1)}, u32[]{:S(2)}, u32[]{:S(2)}) collective-permute-start(bf16[8,1536]{1,0:T(8,128)(2,1)} %param.8), channel_id=1, source_target_pairs={{0,2},{2,0},{1,3},{3,1},{4,6},{6,4},{5,7},{7,5},{8,10},{10,8},{9,1... | collective-permute-start | bytes 73736 | tf_op jit(solution)/shard_map/ppermute | solution.py:35
  5.5 0.8 fusion.18
  6.3 0.7 slice.88
  7.0 0.8 fusion.19
  7.8 0.7 constant_dynamic-update-slice_fusion.5
  8.5 0.7 constant_dynamic-update-slice_fusion.4
  9.2 0.8 pad_maximum_fusion.6
  10.1 0.0 copy-start.3
  10.1 0.0 copy-start.2
  10.1 27.3 %all-gather = bf16[768,640]{1,0:T(8,128)(2,1)S(1)} all-gather(bf16[96,640]{1,0:T(8,128)(2,1)S(1)} %pad_maximum_fusion.6), channel_id=2, replica_groups=mesh['xl'=2,'z'=8,'y2'=4,'y1'=2,'xh'=2,'c'=2] {'z'}, dimensions={0}, use_global_device_ids=true | all-gather | bytes 1105920 | tf_op jit(solution)/shard_map/all_gather | solution.py:149
  37.4 2.2 %collective-permute-start.3 = (bf16[8,96,640]{2,1,0:T(8,128)(2,1)S(1)}, bf16[8,96,640]{2,1,0:T(8,128)(2,1)S(1)}, u32[]{:S(2)}, u32[]{:S(2)}) collective-permute-start(bf16[8,96,640]{2,1,0:T(8,128)(2,1)S(1)} %bitcast.29), channel_id=1, source_target_pairs={{0,256},{256,0},{1,257},{257,1},{2,258},{258,2},{3,259},{259,3},{4... | collective-permute-start | bytes 2949128 | tf_op jit(solution)/shard_map/ppermute | solution.py:35
  39.7 0.1 add_add_fusion
  39.8 0.1 reshape.386
  40.0 0.1 iota_compare_fusion
  40.1 0.2 select_reduce_fusion
  40.3 0.0 collective-permute-done
  40.4 0.9 broadcast_in_dim.74
  41.3 6.9 %all-to-all-start = ((bf16[4,112,640]{2,1,0:T(8,128)(2,1)}), bf16[4,112,640]{2,1,0:T(8,128)(2,1)S(1)}, u32[]{:S(2)}, u32[]{:S(2)}) async-start(bf16[4,112,640]{2,1,0:T(8,128)(2,1)} %broadcast_in_dim.74), calls=%async_computation | async-start | bytes 1146880 | tf_op jit(solution)/shard_map/all_to_all | solution.py:159
  48.3 0.9 slice.120
  49.2 0.1 select_reduce_fusion.1
  49.3 9.4 %all-to-all-done = bf16[4,112,640]{2,1,0:T(8,128)(2,1)S(1)} async-done(((bf16[4,112,640]{2,1,0:T(8,128)(2,1)}), bf16[4,112,640]{2,1,0:T(8,128)(2,1)S(1)}, u32[]{:S(2)}, u32[]{:S(2)}) %all-to-all-start) | async-done | bytes 573472 | tf_op jit(solution)/shard_map/all_to_all | solution.py:159
  58.7 2.1 %collective-permute-start.1 = (bf16[4,48,512]{2,1,0:T(8,128)(2,1)S(1)}, bf16[4,48,512]{2,1,0:T(8,128)(2,1)}, u32[]{:S(2)}, u32[]{:S(2)}) collective-permute-start(bf16[4,48,512]{2,1,0:T(8,128)(2,1)S(1)} %slice.115), channel_id=1, source_target_pairs={{0,4},{4,0},{1,5},{5,1},{2,6},{6,2},{3,7},{7,3},{8,12},{12,8},{9,1... | collective-permute-start | bytes 589832 | tf_op jit(solution)/shard_map/ppermute | solution.py:35
  60.8 0.1 copy.19.refs_10_
  60.9 3.2 %collective-permute-start.4 = (bf16[256,640]{1,0:T(8,128)(2,1)S(1)}, bf16[256,640]{1,0:T(8,128)(2,1)}, u32[]{:S(2)}, u32[]{:S(2)}) collective-permute-start(bf16[256,640]{1,0:T(8,128)(2,1)S(1)} %bitcast.34), channel_id=1, source_target_pairs={{0,4},{4,0},{1,5},{5,1},{2,6},{6,2},{3,7},{7,3},{8,12},{12,8},{9,1... | collective-permute-start | bytes 983048 | tf_op jit(solution)/shard_map/ppermute | solution.py:35
  64.2 3.6 %collective-permute-start.6 = (bf16[256,640]{1,0:T(8,128)(2,1)S(1)}, bf16[256,640]{1,0:T(8,128)(2,1)}, u32[]{:S(2)}, u32[]{:S(2)}) collective-permute-start(bf16[256,640]{1,0:T(8,128)(2,1)S(1)} %bitcast.35), channel_id=1, source_target_pairs={{0,2},{2,0},{1,3},{3,1},{4,6},{6,4},{5,7},{7,5},{8,10},{10,8},{9,1... | collective-permute-start | bytes 983048 | tf_op jit(solution)/shard_map/ppermute | solution.py:35
  67.8 0.0 collective-permute-done.1
  67.8 1.0 broadcast_select_fusion.1
  68.9 0.3 copy.17
  69.2 0.5 broadcast_in_dim_reshape.3
  69.8 13.9 %collective-permute-start.2 = (bf16[16,8,1536]{2,1,0:T(8,128)(2,1)S(1)}, bf16[16,8,1536]{2,1,0:T(8,128)(2,1)S(1)}, u32[]{:S(2)}, u32[]{:S(2)}) collective-permute-start(bf16[16,8,1536]{2,1,0:T(8,128)(2,1)S(1)} %broadcast_in_dim_reshape.3), channel_id=1, source_target_pairs={{0,1},{1,0},{2,3},{3,2},{4,5},{5,4},{6,7},{7,6},{8,9},{9,8},{10,11... | collective-permute-start | bytes 1179656 | tf_op jit(solution)/shard_map/ppermute | solution.py:35
  83.7 0.0 collective-permute-done.3
  83.8 0.9 copy-done
  84.7 0.0 collective-permute-done.4
  84.7 1.0 pad_maximum_fusion.1.refs_0_
  85.8 1.9 %collective-permute-start.5 = (bf16[512,640]{1,0:T(8,128)(2,1)S(1)}, bf16[512,640]{1,0:T(8,128)(2,1)S(1)}, u32[]{:S(2)}, u32[]{:S(2)}) collective-permute-start(bf16[512,640]{1,0:T(8,128)(2,1)S(1)} %pad_maximum_fusion.1.refs_0_), channel_id=1, source_target_pairs={{0,256},{256,0},{1,257},{257,1},{2,258},{258,2},{3,259},{259,3},{4... | collective-permute-start | bytes 1966088 | tf_op jit(solution)/shard_map/ppermute | solution.py:35
  87.7 3.7 %collective-permute-start.8 = (bf16[512,640]{1,0:T(8,128)(2,1)S(1)}, bf16[512,640]{1,0:T(8,128)(2,1)S(1)}, u32[]{:S(2)}, u32[]{:S(2)}) collective-permute-start(bf16[512,640]{1,0:T(8,128)(2,1)S(1)} %pad_maximum_fusion.1.refs_0_), channel_id=1, source_target_pairs={{0,258},{258,0},{2,256},{256,2},{1,259},{259,1},{3,257},{257,3},{4... | collective-permute-start | bytes 1966088 | tf_op jit(solution)/shard_map/ppermute | solution.py:168
  91.4 2.2 %collective-permute-start.9 = (bf16[512,640]{1,0:T(8,128)(2,1)S(1)}, bf16[512,640]{1,0:T(8,128)(2,1)S(1)}, u32[]{:S(2)}, u32[]{:S(2)}) collective-permute-start(bf16[512,640]{1,0:T(8,128)(2,1)S(1)} %pad_maximum_fusion.1.refs_0_), channel_id=1, source_target_pairs={{0,1},{1,0},{2,3},{3,2},{4,5},{5,4},{6,7},{7,6},{8,9},{9,8},{10,11... | collective-permute-start | bytes 1966088 | tf_op jit(solution)/shard_map/ppermute | solution.py:35
  93.6 0.0 collective-permute-done.6
  93.6 1.9 %collective-permute-start.7 = (bf16[256,640]{1,0:T(8,128)(2,1)}, bf16[256,640]{1,0:T(8,128)(2,1)S(1)}, u32[]{:S(2)}, u32[]{:S(2)}) collective-permute-start(bf16[256,640]{1,0:T(8,128)(2,1)} %collective-permute-done.6), channel_id=1, source_target_pairs={{0,4},{4,0},{1,5},{5,1},{2,6},{6,2},{3,7},{7,3},{8,12},{12,8},{9,1... | collective-permute-start | bytes 983048 | tf_op jit(solution)/shard_map/ppermute | solution.py:35
  95.6 1.0 constant_dynamic-update-slice_fusion.7
  96.6 0.0 collective-permute-done.2
  96.6 0.1 select_bitcast_fusion.1
  96.7 0.1 pad_maximum_fusion
  96.8 0.1 copy.18
  96.8 0.0 slice-start
  96.9 1.0 copy-done.1
  97.8 0.4 fusion.2
  98.2 0.4 fusion
  98.6 6.3 %collective-permute-done.7 = bf16[256,640]{1,0:T(8,128)(2,1)S(1)} collective-permute-done((bf16[256,640]{1,0:T(8,128)(2,1)}, bf16[256,640]{1,0:T(8,128)(2,1)S(1)}, u32[]{:S(2)}, u32[]{:S(2)}) %collective-permute-start.7) | collective-permute-done | bytes 327712 | tf_op jit(solution)/shard_map/ppermute | solution.py:35
  104.9 2.9 %collective-permute-start.11 = (bf16[512,640]{1,0:T(8,128)(2,1)S(1)}, bf16[512,640]{1,0:T(8,128)(2,1)S(1)}, u32[]{:S(2)}, u32[]{:S(2)}) collective-permute-start(bf16[512,640]{1,0:T(8,128)(2,1)S(1)} %constant_dynamic-update-slice_fusion.6.refs_2_), channel_id=1, source_target_pairs={{0,1},{1,0},{2,3},{3,2},{4,5},{5,4},{6,7},{7,6},{8,9},{9,8},{10,11... | collective-permute-start | bytes 1966088 | tf_op jit(solution)/shard_map/ppermute | solution.py:35
  107.8 0.0 collective-permute-done.5.refs_1_
  107.8 1.9 %collective-permute-start.10 = (bf16[512,640]{1,0:T(8,128)(2,1)S(1)}, bf16[512,640]{1,0:T(8,128)(2,1)S(1)}, u32[]{:S(2)}, u32[]{:S(2)}) collective-permute-start(bf16[512,640]{1,0:T(8,128)(2,1)S(1)} %collective-permute-done.5.refs_1_), channel_id=1, source_target_pairs={{0,1},{1,0},{2,3},{3,2},{4,5},{5,4},{6,7},{7,6},{8,9},{9,8},{10,11... | collective-permute-start | bytes 1966088 | tf_op jit(solution)/shard_map/ppermute | solution.py:35
  109.8 0.0 collective-permute-done.8.refs_3_
  109.8 2.4 %collective-permute-start.12 = (bf16[512,640]{1,0:T(8,128)(2,1)S(1)}, bf16[512,640]{1,0:T(8,128)(2,1)S(1)}, u32[]{:S(2)}, u32[]{:S(2)}) collective-permute-start(bf16[512,640]{1,0:T(8,128)(2,1)S(1)} %collective-permute-done.8.refs_3_), channel_id=1, source_target_pairs={{0,1},{1,0},{2,3},{3,2},{4,5},{5,4},{6,7},{7,6},{8,9},{9,8},{10,11... | collective-permute-start | bytes 1966088 | tf_op jit(solution)/shard_map/ppermute | solution.py:35
  112.2 0.1 fusion.25
  112.3 0.2 convolution_convert_fusion.1
  112.5 0.2 convolution_convert_fusion
  112.8 0.1 maximum_maximum_fusion.q_ref
  112.9 0.0 collective-permute-done.9.refs_4_
  112.9 0.0 collective-permute-done.11.refs_6_
  112.9 0.0 collective-permute-done.10.refs_5_
  112.9 1.0 collective-permute-done.12.refs_7_
  113.9 0.9 copy-done.5
  114.8 9.4 %shard_map.82 = bf16[256,256]{1,0:T(8,128)(2,1)} custom-call(bf16[512,640]{1,0:T(8,128)(2,1)S(1)} %maximum_maximum_fusion.q_ref, bf16[512,640]{1,0:T(8,128)(2,1)S(1)} %pad_maximum_fusion.1.refs_0_, bf16[512,640]{1,0:T(8,128)(2,1)S(1)} %collective-permute-done.5.refs_1_, bf16[512,640]{1,0:T(8,128)(2,1)S(1)} %constant_dynamic-update-slice_fusion.6.refs_2_, ...), custom_call_target="tpu_custom_call" | custom-call | flops 4563402752 | bytes 5242880 | tf_op jit(solution)/shard_map/pallas_call | solution.py:112
  (34 shorter events, 0.4 us)
Async XLA Ops:
  0.0 40.3 %collective-permute-start = (bf16[8,1536]{1,0:T(8,128)(2,1)}, bf16[8,1536]{1,0:T(8,128)(2,1)S(1)}, u32[]{:S(2)}, u32[]{:S(2)}) collective-permute-start(bf16[8,1536]{1,0:T(8,128)(2,1)} %param.8), channel_id=1, source_target_pairs={{0,2},{2,0},{1,3},{3,1},{4,6},{6,4},{5,7},{7,5},{8,10},{10,8},{9,1... | collective-permute-start | bytes 73736 | tf_op jit(solution)/shard_map/ppermute | solution.py:35
  10.1 30.0 %copy-start.3 = (s32[2,32]{1,0:T(2,128)S(1)}, s32[2,32]{1,0:T(2,128)}, u32[]{:S(2)}) copy-start(s32[2,32]{1,0:T(2,128)} %param.15) | copy-start | bytes 772
  10.1 30.3 %copy-start.2 = (bf16[8,1536]{1,0:T(8,128)(2,1)S(1)}, bf16[8,1536]{1,0:T(8,128)(2,1)}, u32[]{:S(2)}) copy-start(bf16[8,1536]{1,0:T(8,128)(2,1)} %param.8) | copy-start | bytes 73732
  37.4 46.3 %collective-permute-start.3 = (bf16[8,96,640]{2,1,0:T(8,128)(2,1)S(1)}, bf16[8,96,640]{2,1,0:T(8,128)(2,1)S(1)}, u32[]{:S(2)}, u32[]{:S(2)}) collective-permute-start(bf16[8,96,640]{2,1,0:T(8,128)(2,1)S(1)} %bitcast.29), channel_id=1, source_target_pairs={{0,256},{256,0},{1,257},{257,1},{2,258},{258,2},{3,259},{259,3},{4... | collective-permute-start | bytes 2949128 | tf_op jit(solution)/shard_map/ppermute | solution.py:35
  41.3 7.9 %copy-start.4 = (s32[24]{0:T(128)S(1)}, s32[24]{0:T(128)}, u32[]{:S(2)}) copy-start(s32[24]{0:T(128)} %param.14) | copy-start | bytes 292
  41.3 17.4 %all-to-all-start = ((bf16[4,112,640]{2,1,0:T(8,128)(2,1)}), bf16[4,112,640]{2,1,0:T(8,128)(2,1)S(1)}, u32[]{:S(2)}, u32[]{:S(2)}) async-start(bf16[4,112,640]{2,1,0:T(8,128)(2,1)} %broadcast_in_dim.74), calls=%async_computation | async-start | bytes 1146880 | tf_op jit(solution)/shard_map/all_to_all | solution.py:159
  58.7 9.2 %collective-permute-start.1 = (bf16[4,48,512]{2,1,0:T(8,128)(2,1)S(1)}, bf16[4,48,512]{2,1,0:T(8,128)(2,1)}, u32[]{:S(2)}, u32[]{:S(2)}) collective-permute-start(bf16[4,48,512]{2,1,0:T(8,128)(2,1)S(1)} %slice.115), channel_id=1, source_target_pairs={{0,4},{4,0},{1,5},{5,1},{2,6},{6,2},{3,7},{7,3},{8,12},{12,8},{9,1... | collective-permute-start | bytes 589832 | tf_op jit(solution)/shard_map/ppermute | solution.py:35
  60.9 23.8 %collective-permute-start.4 = (bf16[256,640]{1,0:T(8,128)(2,1)S(1)}, bf16[256,640]{1,0:T(8,128)(2,1)}, u32[]{:S(2)}, u32[]{:S(2)}) collective-permute-start(bf16[256,640]{1,0:T(8,128)(2,1)S(1)} %bitcast.34), channel_id=1, source_target_pairs={{0,4},{4,0},{1,5},{5,1},{2,6},{6,2},{3,7},{7,3},{8,12},{12,8},{9,1... | collective-permute-start | bytes 983048 | tf_op jit(solution)/shard_map/ppermute | solution.py:35
  64.2 29.5 %collective-permute-start.6 = (bf16[256,640]{1,0:T(8,128)(2,1)S(1)}, bf16[256,640]{1,0:T(8,128)(2,1)}, u32[]{:S(2)}, u32[]{:S(2)}) collective-permute-start(bf16[256,640]{1,0:T(8,128)(2,1)S(1)} %bitcast.35), channel_id=1, source_target_pairs={{0,2},{2,0},{1,3},{3,1},{4,6},{6,4},{5,7},{7,5},{8,10},{10,8},{9,1... | collective-permute-start | bytes 983048 | tf_op jit(solution)/shard_map/ppermute | solution.py:35
  69.8 26.8 %collective-permute-start.2 = (bf16[16,8,1536]{2,1,0:T(8,128)(2,1)S(1)}, bf16[16,8,1536]{2,1,0:T(8,128)(2,1)S(1)}, u32[]{:S(2)}, u32[]{:S(2)}) collective-permute-start(bf16[16,8,1536]{2,1,0:T(8,128)(2,1)S(1)} %broadcast_in_dim_reshape.3), channel_id=1, source_target_pairs={{0,1},{1,0},{2,3},{3,2},{4,5},{5,4},{6,7},{7,6},{8,9},{9,8},{10,11... | collective-permute-start | bytes 1179656 | tf_op jit(solution)/shard_map/ppermute | solution.py:35
  83.7 1.0 copy-start
  85.8 22.1 %collective-permute-start.5 = (bf16[512,640]{1,0:T(8,128)(2,1)S(1)}, bf16[512,640]{1,0:T(8,128)(2,1)S(1)}, u32[]{:S(2)}, u32[]{:S(2)}) collective-permute-start(bf16[512,640]{1,0:T(8,128)(2,1)S(1)} %pad_maximum_fusion.1.refs_0_), channel_id=1, source_target_pairs={{0,256},{256,0},{1,257},{257,1},{2,258},{258,2},{3,259},{259,3},{4... | collective-permute-start | bytes 1966088 | tf_op jit(solution)/shard_map/ppermute | solution.py:35
  87.7 22.1 %collective-permute-start.8 = (bf16[512,640]{1,0:T(8,128)(2,1)S(1)}, bf16[512,640]{1,0:T(8,128)(2,1)S(1)}, u32[]{:S(2)}, u32[]{:S(2)}) collective-permute-start(bf16[512,640]{1,0:T(8,128)(2,1)S(1)} %pad_maximum_fusion.1.refs_0_), channel_id=1, source_target_pairs={{0,258},{258,0},{2,256},{256,2},{1,259},{259,1},{3,257},{257,3},{4... | collective-permute-start | bytes 1966088 | tf_op jit(solution)/shard_map/ppermute | solution.py:168
  91.4 21.5 %collective-permute-start.9 = (bf16[512,640]{1,0:T(8,128)(2,1)S(1)}, bf16[512,640]{1,0:T(8,128)(2,1)S(1)}, u32[]{:S(2)}, u32[]{:S(2)}) collective-permute-start(bf16[512,640]{1,0:T(8,128)(2,1)S(1)} %pad_maximum_fusion.1.refs_0_), channel_id=1, source_target_pairs={{0,1},{1,0},{2,3},{3,2},{4,5},{5,4},{6,7},{7,6},{8,9},{9,8},{10,11... | collective-permute-start | bytes 1966088 | tf_op jit(solution)/shard_map/ppermute | solution.py:35
  93.6 11.2 %collective-permute-start.7 = (bf16[256,640]{1,0:T(8,128)(2,1)}, bf16[256,640]{1,0:T(8,128)(2,1)S(1)}, u32[]{:S(2)}, u32[]{:S(2)}) collective-permute-start(bf16[256,640]{1,0:T(8,128)(2,1)} %collective-permute-done.6), channel_id=1, source_target_pairs={{0,4},{4,0},{1,5},{5,1},{2,6},{6,2},{3,7},{7,3},{8,12},{12,8},{9,1... | collective-permute-start | bytes 983048 | tf_op jit(solution)/shard_map/ppermute | solution.py:35
  96.8 1.1 copy-start.1
  96.8 1.3 %slice-start = ((bf16[8,96,640]{2,1,0:T(8,128)(2,1)}), bf16[8,96,384]{2,1,0:T(8,128)(2,1)S(1)}, s32[]{:S(2)}) async-start(bf16[8,96,640]{2,1,0:T(8,128)(2,1)} %copy-done), calls=%async_computation.1 | async-start | bytes 1179648 | tf_op jit(solution)/shard_map/slice | solution.py:184
  104.9 8.0 %collective-permute-start.11 = (bf16[512,640]{1,0:T(8,128)(2,1)S(1)}, bf16[512,640]{1,0:T(8,128)(2,1)S(1)}, u32[]{:S(2)}, u32[]{:S(2)}) collective-permute-start(bf16[512,640]{1,0:T(8,128)(2,1)S(1)} %constant_dynamic-update-slice_fusion.6.refs_2_), channel_id=1, source_target_pairs={{0,1},{1,0},{2,3},{3,2},{4,5},{5,4},{6,7},{7,6},{8,9},{9,8},{10,11... | collective-permute-start | bytes 1966088 | tf_op jit(solution)/shard_map/ppermute | solution.py:35
  107.8 5.1 %collective-permute-start.10 = (bf16[512,640]{1,0:T(8,128)(2,1)S(1)}, bf16[512,640]{1,0:T(8,128)(2,1)S(1)}, u32[]{:S(2)}, u32[]{:S(2)}) collective-permute-start(bf16[512,640]{1,0:T(8,128)(2,1)S(1)} %collective-permute-done.5.refs_1_), channel_id=1, source_target_pairs={{0,1},{1,0},{2,3},{3,2},{4,5},{5,4},{6,7},{7,6},{8,9},{9,8},{10,11... | collective-permute-start | bytes 1966088 | tf_op jit(solution)/shard_map/ppermute | solution.py:35
  109.8 4.1 %collective-permute-start.12 = (bf16[512,640]{1,0:T(8,128)(2,1)S(1)}, bf16[512,640]{1,0:T(8,128)(2,1)S(1)}, u32[]{:S(2)}, u32[]{:S(2)}) collective-permute-start(bf16[512,640]{1,0:T(8,128)(2,1)S(1)} %collective-permute-done.8.refs_3_), channel_id=1, source_target_pairs={{0,1},{1,0},{2,3},{3,2},{4,5},{5,4},{6,7},{7,6},{8,9},{9,8},{10,11... | collective-permute-start | bytes 1966088 | tf_op jit(solution)/shard_map/ppermute | solution.py:35
  113.9 0.9 copy-start.5

commit v2 on v1

v2 whole, which is shorter than its diff:
```python
import jax
import jax.numpy as jnp
import numpy as np
from jax import lax
from jax.experimental import pallas as pl
from jax.experimental.pallas import tpu as pltpu
from jax.sharding import Mesh, PartitionSpec as P

LATENT_WIDTH = 512
ROTARY_DIMS = 64
PLAIN_QUERY_DIMS = 128
VALUE_DIMS = 128
TILE = 128
WIDTH = 640
KEY_STEP = 512
SCALE = (PLAIN_QUERY_DIMS + ROTARY_DIMS) ** (-0.5)
FACTOR = SCALE * 1.4426950408889634
NEG = -1e30
FLOOR = -1e29

AXES = ("xl", "z2", "z1", "y2", "y1", "xh", "c")
SIZES = (2, 4, 2, 4, 2, 2, 2)
Z = ("z2", "z1")
BLK = ("xl", "z2", "z1")
WIDE = ("y2", "y1", "xh", "c")


def prepare_kernel(kv_ref, wp_ref, wr_ref, ku_ref, vu_ref, kv_out, w_out):
    raw = kv_ref[...].astype(jnp.float32)
    latent = raw[:, :LATENT_WIDTH]
    energy = jnp.mean(latent * latent, axis=1, keepdims=True)
    normed = (latent * lax.rsqrt(energy + 1e-06)).astype(jnp.bfloat16)
    rope = raw[:, LATENT_WIDTH:]
    rope = jnp.concatenate([rope, jnp.zeros_like(rope)], axis=1).astype(jnp.bfloat16)
    for copy in range(kv_out.shape[0]):
        kv_out[copy, :, 0:LATENT_WIDTH] = normed
        kv_out[copy, :, LATENT_WIDTH:WIDTH] = rope
    w_out[0:96, 0:256] = wp_ref[...]
    w_out[0:96, 256:384] = wr_ref[...]
    w_out[0:32, 384:512] = ku_ref[:, 0:128]
    w_out[32:64, 384:512] = ku_ref[:, 128:256]
    w_out[64:96, 384:512] = vu_ref[:, 0:128]
    w_out[96:112, 0:128] = vu_ref[0:16, 128:256]
    w_out[96:112, 128:256] = vu_ref[16:32, 128:256]
    w_out[96:112, 256:512] = jnp.zeros((16, 256), jnp.bfloat16)


def prepare(kv_raw, wp, wr, ku, vu):
    vmem = pl.BlockSpec(memory_space=pltpu.VMEM)
    return pl.pallas_call(
        prepare_kernel,
        out_shape=(
            jax.ShapeDtypeStruct((32, 8, WIDTH), jnp.bfloat16),
            jax.ShapeDtypeStruct((112, 512), jnp.bfloat16),
        ),
        in_specs=[vmem] * 5,
        out_specs=(vmem, vmem),
    )(kv_raw, wp, wr, ku, vu)


def swap(x, axis):
    return lax.ppermute(x, axis, [(0, 1), (1, 0)])


def in_order(bit, own, other, axis):
    first = jnp.where(bit == 0, own, other)
    second = jnp.where(bit == 0, other, own)
    return jnp.concatenate([first, second], axis=axis)


def gather_direct(x, axes, members):
    return lax.all_to_all(jnp.broadcast_to(x[None], (members,) + x.shape), axes, 0, 0)


def project_kernel(core_ref, mine_ref, other_ref, w_ref, q_out, vu_out):
    def rows_of(first, many, cols):
        parts = [w_ref[:, half, first : first + many, cols] for half in range(2)]
        return [part.reshape(8 * many, part.shape[-1]) for part in parts]

    low, high = rows_of(0, 96, slice(0, 384))

    def product(ref):
        return jnp.dot(ref[:, 0:768], low, preferred_element_type=jnp.float32) + jnp.dot(
            ref[:, 768:1536], high, preferred_element_type=jnp.float32
        )

    mine, other = product(mine_ref), product(other_ref)
    is_first = core_ref[0] == 0
    parts = [jnp.where(is_first, mine, other), jnp.where(is_first, other, mine)]
    projected = jnp.stack([part.reshape(16, 8, 384) for part in parts], axis=1).reshape(256, 384)
    for head in range(2):
        nope = projected[:, head * 128 : head * 128 + 128].astype(jnp.bfloat16)
        rope = projected[:, 256 + head * 64 : 320 + head * 64]
        key_up = jnp.concatenate(rows_of(32 * head, 32, slice(384, 512)), axis=0)
        absorbed = lax.dot_general(nope, key_up, (((1,), (1,)), ((), ())), preferred_element_type=jnp.float32)
        at = pl.ds(head * 256, 256)
        q_out[at, 0:LATENT_WIDTH] = absorbed.astype(jnp.bfloat16)
        q_out[at, LATENT_WIDTH:WIDTH] = jnp.concatenate([rope, jnp.zeros_like(rope)], axis=1).astype(jnp.bfloat16)
    vu_out[:, 0:128] = jnp.concatenate(rows_of(64, 32, slice(384, 512)), axis=0)
    for half in range(2):
        upper = [w_ref[:, half, 96:112, 128 * j : 128 * j + 128] for j in range(2)]
        vu_out[pl.ds(half * 256, 256), 128:256] = jnp.concatenate(upper, axis=1).reshape(256, 128)


def project(core, mine, other, weights):
    vmem = pl.BlockSpec(memory_space=pltpu.VMEM)
    return pl.pallas_call(
        project_kernel,
        out_shape=(
            jax.ShapeDtypeStruct((512, WIDTH), jnp.bfloat16),
            jax.ShapeDtypeStruct((512, 256), jnp.bfloat16),
        ),
        in_specs=[pl.BlockSpec(memory_space=pltpu.SMEM)] + [vmem] * 3,
        out_specs=(vmem, vmem),
        compiler_params=pltpu.CompilerParams(vmem_limit_bytes=32 * 1024 * 1024),
    )(core.reshape(1), mine, other, weights)


def attend(q_ref, keys_refs, low_ref, high_ref, bounds_ref, s_ref, peaks):
    q = q_ref[...]
    rows = q.shape[0]
    steps = []
    for keys_ref in keys_refs:
        for start in range(0, keys_ref.shape[0], KEY_STEP):
            steps.append((len(steps) * KEY_STEP, keys_ref, start))
    groups = rows // TILE
    half = groups // 2
    highest = [jnp.full((TILE, 128), FLOOR, jnp.float32) for _ in range(groups)]
    for at, keys_ref, start in steps:
        keys = keys_ref[pl.ds(start, KEY_STEP), :]
        scores = lax.dot_general(
            q, keys, (((1,), (1,)), ((), ())), preferred_element_type=jnp.float32
        )
        for tile in range(half):
            last = bounds_ref[pl.ds(tile * TILE, TILE), 0:1]
            first = bounds_ref[pl.ds(tile * TILE, TILE), 1:2]
            low = low_ref[tile : tile + 1, pl.ds(at, KEY_STEP)]
            high = high_ref[tile : tile + 1, pl.ds(at, KEY_STEP)]
            allowed = (low <= last) & (high >= first)
            for head in range(2):
                g = head * half + tile
                part = jnp.where(allowed, scores[g * TILE : (g + 1) * TILE, :], NEG)
                s_ref[pl.ds(g * TILE, TILE), pl.ds(at, KEY_STEP)] = part
                top = highest[g]
                for lane in range(0, KEY_STEP, 128):
                    top = jnp.maximum(top, part[:, lane : lane + 128])
                highest[g] = top
    found = [jnp.max(h, axis=1, keepdims=True) for h in highest]
    if peaks is not None:
        found = [jnp.maximum(new, old) for new, old in zip(found, peaks)]
    sums = [jnp.zeros((TILE, 128), jnp.float32) for _ in range(groups)]
    accum = jnp.zeros((rows, LATENT_WIDTH), jnp.float32)
    for at, keys_ref, start in steps:
        parts = []
        for g in range(groups):
            part = s_ref[pl.ds(g * TILE, TILE), pl.ds(at, KEY_STEP)]
            weights = jnp.exp2((part - found[g]) * FACTOR)
            total = sums[g]
            for lane in range(0, KEY_STEP, 128):
                total = total + weights[:, lane : lane + 128]
            sums[g] = total
            parts.append(weights.astype(jnp.bfloat16))
        accum = accum + jnp.dot(
            jnp.concatenate(parts, axis=0),
            keys_ref[pl.ds(start, KEY_STEP), 0:LATENT_WIDTH],
            preferred_element_type=jnp.float32,
        )
    return [jnp.sum(s, axis=1, keepdims=True) for s in sums], found, accum


def first_half_kernel(*refs):
    q_ref, *keys_refs = refs[:-7]
    low_ref, high_ref, bounds_ref, accum_ref, sums_ref, peaks_ref, s_ref = refs[-7:]
    sums, peaks, accum = attend(q_ref, keys_refs, low_ref, high_ref, bounds_ref, s_ref, None)
    accum_ref[...] = accum
    for g in range(len(sums)):
        sums_ref[pl.ds(g * TILE, TILE), :] = jnp.broadcast_to(sums[g], (TILE, 128))
        peaks_ref[pl.ds(g * TILE, TILE), :] = jnp.broadcast_to(peaks[g], (TILE, 128))


def second_half_kernel(*refs):
    q_ref, *keys_refs = refs[:-9]
    low_ref, high_ref, bounds_ref, accum_ref, sums_ref, peaks_ref, vu_ref, o_ref, s_ref = refs[-9:]
    groups = q_ref.shape[0] // TILE
    half = groups // 2
    old = [peaks_ref[pl.ds(g * TILE, TILE), 0:1] for g in range(groups)]
    sums, peaks, accum = attend(q_ref, keys_refs, low_ref, high_ref, bounds_ref, s_ref, old)
    latent_out = []
    for g in range(groups):
        rows = pl.ds(g * TILE, TILE)
        carry = jnp.exp2((old[g] - peaks[g]) * FACTOR)
        total = sums[g] + sums_ref[rows, 0:1] * carry
        summed = accum[g * TILE : (g + 1) * TILE, :] + accum_ref[rows, :] * carry
        latent_out.append((summed * (1.0 / total)).astype(jnp.bfloat16))
    for head in range(2):
        cols = pl.ds(head * VALUE_DIMS, VALUE_DIMS)
        o_ref[:, cols] = jnp.dot(
            jnp.concatenate(latent_out[head * half : (head + 1) * half], axis=0),
            vu_ref[:, cols],
            preferred_element_type=jnp.float32,
        ).astype(jnp.bfloat16)


def attention(query, mine, theirs, low, high, bounds, value_up):
    rows, count = query.shape[0], low.shape[1] // 2
    vmem = pl.BlockSpec(memory_space=pltpu.VMEM)
    common = dict(
        scratch_shapes=[pltpu.VMEM((rows, count), jnp.float32)],
        compiler_params=pltpu.CompilerParams(vmem_limit_bytes=32 * 1024 * 1024),
        cost_estimate=pl.CostEstimate(
            flops=2 * rows * count * (576 + 512), bytes_accessed=count * WIDTH * 2, transcendentals=rows * count
        ),
    )
    state = pl.pallas_call(
        first_half_kernel,
        out_shape=(
            jax.ShapeDtypeStruct((rows, LATENT_WIDTH), jnp.float32),
            jax.ShapeDtypeStruct((rows, 128), jnp.float32),
            jax.ShapeDtypeStruct((rows, 128), jnp.float32),
        ),
        in_specs=[vmem] * (4 + len(mine)),
        out_specs=(vmem,) * 3,
        **common,
    )(query, *mine, low[:, :count], high[:, :count], bounds)
    return pl.pallas_call(
        second_half_kernel,
        out_shape=jax.ShapeDtypeStruct((rows // 2, 2 * VALUE_DIMS), jnp.bfloat16),
        in_specs=[vmem] * (8 + len(theirs)),
        out_specs=vmem,
        **common,
    )(query, *theirs, low[:, count:], high[:, count:], bounds, *state, value_up)


def body(
    q_latent,
    kv_raw,
    query_plain_weight,
    query_rotary_weight,
    key_up_weight,
    value_up_weight,
    doc_starts,
    tile_kind,
):
    xl, z2, z1 = lax.axis_index("xl"), lax.axis_index("z2"), lax.axis_index("z1")
    y1, xh, core = lax.axis_index("y1"), lax.axis_index("xh"), lax.axis_index("c")

    kv, packed = prepare(kv_raw, query_plain_weight, query_rotary_weight, key_up_weight, value_up_weight)

    kv, packed, q_latent = lax.optimization_barrier((kv, packed, q_latent))
    w_pair = in_order(xl, packed[None], swap(packed, "xl")[None], 0)
    q_pair = in_order(xh, q_latent[None], swap(q_latent, "xh")[None], 0)

    near = lax.all_to_all(kv, (*Z, "y2"), 0, 0).reshape(256, WIDTH)
    weights = lax.all_gather(w_pair, Z)

    q_pair, near = lax.optimization_barrier((q_pair, near))
    q_half = gather_direct(q_pair, ("y2", "y1"), 8)
    q_core = swap(q_half, "c")

    next_y = swap(near, "y1")
    x2_near = swap(near, "xh")
    pair = jnp.concatenate([near, next_y], axis=0)
    x1_pair = swap(pair, "xl")
    x3_pair = lax.ppermute(pair, ("xl", "xh"), [(0, 3), (3, 0), (1, 2), (2, 1)])
    x2_far, pair = lax.optimization_barrier((x2_near, pair))
    x2_next = swap(x2_far, "y1")
    x2_pair = jnp.concatenate([x2_near, x2_next], axis=0)

    query, value_up = project(core, q_half.reshape(128, 1536), q_core.reshape(128, 1536), weights)

    x1_pair, x3_pair, query = lax.optimization_barrier((x1_pair, x3_pair, query))
    mine = [pair, x1_pair, x2_pair, x3_pair]
    theirs = [swap(piece, "c") for piece in mine]

    shape = (2, 4, 2, 8, 4, 8)
    at = lambda d: lax.broadcasted_iota(jnp.int32, shape, d)
    far = at(1)
    k_xl, k_xh = xl ^ (far & 1), xh ^ (far >> 1)
    k_block = k_xl * 8 + at(3)
    k_y = 2 * at(4) + (y1 ^ at(2))
    k_pos = (k_block * 256 + ((k_y * 2 + k_xh) * 2 + (core ^ at(0))) * 8 + at(5)).reshape(1, 4096)
    k_tile = k_pos // TILE
    kinds = jnp.sum(
        jnp.where(
            lax.broadcasted_iota(jnp.int32, (1, 32, 4096), 1) == k_tile[:, None, :], tile_kind[:, :, None], 0
        ),
        axis=1,
    )
    big = jnp.int32(1 << 20)
    low = jnp.where(kinds == 2, k_pos, jnp.where(kinds == 1, -1, big))
    high = jnp.where(kinds == 2, k_pos, jnp.where(kinds == 1, big, -1))
    q_pos = (xl * 8 + 2 * z2 + z1) * 256 + lax.broadcasted_iota(jnp.int32, (256, 1), 0)
    q_first = jnp.max(jnp.where(doc_starts[None, :] <= q_pos, doc_starts[None, :], 0), axis=1, keepdims=True)
    bounds = jnp.concatenate([q_pos, q_first], axis=1)
    return attention(query, mine, theirs, low, high, bounds, value_up)


def solution(mesh):
    fine = Mesh(np.asarray(mesh.devices).reshape(SIZES), AXES)
    return jax.shard_map(
        body,
        mesh=fine,
        in_specs=(
            P(AXES, None),
            P(AXES, None),
            P(BLK, WIDE),
            P(BLK, WIDE),
            P(BLK, WIDE),
            P(BLK, WIDE),
            P(),
            P(BLK, None),
        ),
        out_specs=P(BLK, WIDE),
        check_vma=False,
    )
```

time: 125 us -> 111 us (0.89)
  blocking collectives: 27.3 us -> 0 us
  between operations: 0.54 us -> 13.8 us
  local copies, waits for them, and re-layouts: 9.08 us -> 3.79 us
  waiting for transfers between devices: 16.7 us -> 20.8 us
  Pallas kernels: 9.39 us -> 13.4 us
  other arithmetic: 5.45 us -> 2.25 us
  starting transfers between devices: 54.5 us -> 56.4 us
    all_gather x1 -> x0, blocking collectives: 27.3 us -> none  [body(): by_z = lax.all_gather(packed, 'z')]
    all_to_all x1 -> x2, starting transfers between devices: 6.95 us -> 21 us  [the longest x1 15.7 us: body(): near = lax.all_to_all(kv, (*Z, 'y2'), 0, 0).reshape(256, WIDTH)]
    ppermute x12 -> x11, starting transfers between devices: 43.9 us -> 32.9 us  [swap(): return lax.ppermute(x, axis, [(0, 1), (1, 0)])]
    ppermute x12 -> x11, waiting for transfers between devices: 7.28 us -> 15.3 us  [swap(): return lax.ppermute(x, axis, [(0, 1), (1, 0)])]
    pallas_call x1 -> x4, Pallas kernels: 9.39 us -> 13.4 us  [the longest x1 6.02 us: attention(): pl.pallas_call(second_half_kernel, out_shape=jax.ShapeDtypeStruct((rows /...]
    all_to_all x1 -> x2, waiting for transfers between devices: 9.39 us -> 5.49 us  [the longest x1 5.48 us: body(): near = lax.all_to_all(kv, (*Z, 'y2'), 0, 0).reshape(256, WIDTH)]
    unnamed x18 -> x10, local copies, waits for them, and re-layouts: 5.21 us -> 1.56 us
    concatenate x4 -> x0, other arithmetic: 1.99 us -> none  [the longest x1 1.03 us: body(): pair = jnp.concatenate([near, next_y], axis=0)]
  transfers between devices with their start and end apart: 14 -> 15, of which waited for: 3 -> 4; matrix products, arithmetic and copies ran while one was open for 10% -> 4% of each run, Pallas kernels for 0% -> 5%
where the time goes in v2:
time: 111 us
  starting transfers between devices  56.4 us (51%)
  waiting for transfers between devices  20.8 us (19%)
  between operations  13.8 us (12%)
  Pallas kernels  13.4 us (12%)
  local copies, waits for them, and re-layouts  3.79 us (3%)
  other arithmetic  2.25 us (2%)
    ppermute x11, starting transfers between devices, swap(): return lax.ppermute(x, axis, [(0, 1), (1, 0)])  32.9 us
    all_to_all x1, starting transfers between devices, body(): near = lax.all_to_all(kv, (*Z, 'y2'), 0, 0).reshape(256, WIDTH)  15.7 us
    ppermute x11, waiting for transfers between devices, swap(): return lax.ppermute(x, axis, [(0, 1), (1, 0)])  15.3 us
    pallas_call x1, Pallas kernels, attention(): pl.pallas_call(second_half_kernel, out_shape=jax.ShapeDtypeStruct((rows /...  6.02 us
    all_to_all x1, waiting for transfers between devices, body(): near = lax.all_to_all(kv, (*Z, 'y2'), 0, 0).reshape(256, WIDTH)  5.48 us
    all_to_all x1, starting transfers between devices, gather_direct(): lax.all_to_all(jnp.broadcast_to(x[None], (members,) + x.shape), axes, 0, 0)  5.29 us
    pallas_call x1, Pallas kernels, attention(): pl.pallas_call(first_half_kernel, out_shape=(jax.ShapeDtypeStruct((rows,...  4.98 us
    ppermute x1, starting transfers between devices, body(): x3_pair = lax.ppermute(pair, ('xl', 'xh'), [(0, 3), (3, 0), (1, 2), (2, 1)])  2.47 us
  transfers between devices with their start and end apart: 15, of which 4 were waited for; matrix products, arithmetic and copies ran while one was open for 4% of the time, Pallas kernels for 5%

profile of v2, /device:TPU:1, one launch (start us, length us, event | category | flops | bytes accessed | tf_op | source)
XLA Modules:
  0.0 110.5 jit_solution(9223950006379083399)
XLA Ops:
  6.5 0.0 copy-start.1
  6.5 0.0 copy-start.2
  6.5 1.6 %shard_map.82 = (bf16[32,8,640]{2,1,0:T(8,128)(2,1)}, bf16[112,512]{1,0:T(8,128)(2,1)}) custom-call(bf16[8,576]{1,0:T(8,128)(2,1)} %kv_ref.1, bf16[96,256]{1,0:T(8,128)(2,1)} %wp_ref.1, bf16[96,128]{1,0:T(8,128)(2,1)} %wr_ref.1, bf16[32,256]{1,0:T(8,128)(2,1)} %ku_ref.1, bf16[32,256]{1,0:T(8,128)(2,1)} %vu_ref.1), custom_call_target="tpu_custom_call" | custom-call | tf_op jit(solution)/shard_map/pallas_call | solution.py:50
  8.2 5.5 %collective-permute-start = (bf16[8,1536]{1,0:T(8,128)(2,1)}, bf16[8,1536]{1,0:T(8,128)(2,1)S(1)}, u32[]{:S(2)}, u32[]{:S(2)}) collective-permute-start(bf16[8,1536]{1,0:T(8,128)(2,1)} %param.8), channel_id=1, source_target_pairs={{0,2},{2,0},{1,3},{3,1},{4,6},{6,4},{5,7},{7,5},{8,10},{10,8},{9,1... | collective-permute-start | bytes 73736 | tf_op jit(solution)/shard_map/ppermute | solution.py:62
  13.7 15.7 %all-to-all-start = ((bf16[32,8,640]{2,1,0:T(8,128)(2,1)}), bf16[32,8,640]{2,1,0:T(8,128)(2,1)S(1)}, u32[]{:S(2)}, u32[]{:S(2)}) async-start(bf16[32,8,640]{2,1,0:T(8,128)(2,1)} %get-tuple-element.25), calls=%async_computation | async-start | bytes 655360 | tf_op jit(solution)/shard_map/all_to_all | solution.py:253
  29.4 0.0 all-gather.3.cloned.1.call-start
  29.4 2.2 %collective-permute-start.5 = (bf16[112,512]{1,0:T(8,128)(2,1)}, bf16[112,512]{1,0:T(8,128)(2,1)S(1)}, u32[]{:S(2)}, u32[]{:S(2)}) collective-permute-start(bf16[112,512]{1,0:T(8,128)(2,1)} %get-tuple-element.28), channel_id=1, source_target_pairs={{0,256},{256,0},{1,257},{257,1},{2,258},{258,2},{3,259},{259,3},{4... | collective-permute-start | bytes 344072 | tf_op jit(solution)/shard_map/ppermute | solution.py:62
  31.7 0.1 add_add_fusion
  31.8 0.2 reshape.345
  32.1 3.4 %collective-permute-done.5 = bf16[112,512]{1,0:T(8,128)(2,1)S(1)} collective-permute-done((bf16[112,512]{1,0:T(8,128)(2,1)}, bf16[112,512]{1,0:T(8,128)(2,1)S(1)}, u32[]{:S(2)}, u32[]{:S(2)}) %collective-permute-start.5) | collective-permute-done | bytes 114720 | tf_op jit(solution)/shard_map/ppermute | solution.py:62
  35.5 0.9 select_bitcast_fusion.1
  36.4 0.7 pad_maximum_fusion
  37.1 0.0 copy-start.3
  37.1 0.0 all-gather.3.cloned.1.call-update
  37.1 0.1 iota_compare_fusion
  37.2 0.0 copy-done.2
  37.2 0.2 select_reduce_fusion
  37.5 0.0 collective-permute-done
  37.5 0.0 copy-done.1
  37.5 5.5 %all-to-all-done = bf16[32,8,640]{2,1,0:T(8,128)(2,1)S(1)} async-done(((bf16[32,8,640]{2,1,0:T(8,128)(2,1)}), bf16[32,8,640]{2,1,0:T(8,128)(2,1)S(1)}, u32[]{:S(2)}, u32[]{:S(2)}) %all-to-all-start) | async-done | bytes 327712 | tf_op jit(solution)/shard_map/all_to_all | solution.py:253
  43.0 0.8 broadcast_in_dim.70
  43.8 5.3 %all-to-all-start.1 = ((bf16[8,2,8,1536]{3,2,1,0:T(8,128)(2,1)}), bf16[8,2,8,1536]{3,2,1,0:T(8,128)(2,1)S(1)}, u32[]{:S(2)}, u32[]{:S(2)}) async-start(bf16[8,2,8,1536]{3,2,1,0:T(8,128)(2,1)} %broadcast_in_dim.70), calls=%async_computation.1 | async-start | bytes 786432 | tf_op jit(solution)/shard_map/all_to_all | solution.py:72
  49.1 3.4 %collective-permute-start.1 = (bf16[256,640]{1,0:T(8,128)(2,1)S(1)}, bf16[256,640]{1,0:T(8,128)(2,1)S(1)}, u32[]{:S(2)}, u32[]{:S(2)}) collective-permute-start(bf16[256,640]{1,0:T(8,128)(2,1)S(1)} %bitcast.17), channel_id=1, source_target_pairs={{0,4},{4,0},{1,5},{5,1},{2,6},{6,2},{3,7},{7,3},{8,12},{12,8},{9,1... | collective-permute-start | bytes 983048 | tf_op jit(solution)/shard_map/ppermute | solution.py:62
  52.5 2.1 %collective-permute-start.6 = (bf16[256,640]{1,0:T(8,128)(2,1)S(1)}, bf16[256,640]{1,0:T(8,128)(2,1)S(1)}, u32[]{:S(2)}, u32[]{:S(2)}) collective-permute-start(bf16[256,640]{1,0:T(8,128)(2,1)S(1)} %bitcast.18), channel_id=1, source_target_pairs={{0,2},{2,0},{1,3},{3,1},{4,6},{6,4},{5,7},{7,5},{8,10},{10,8},{9,1... | collective-permute-start | bytes 983048 | tf_op jit(solution)/shard_map/ppermute | solution.py:62
  54.7 11.3 %collective-permute-done.1 = bf16[256,640]{1,0:T(8,128)(2,1)S(1)} collective-permute-done((bf16[256,640]{1,0:T(8,128)(2,1)S(1)}, bf16[256,640]{1,0:T(8,128)(2,1)S(1)}, u32[]{:S(2)}, u32[]{:S(2)}) %collective-permute-start.1) | collective-permute-done | bytes 327712 | tf_op jit(solution)/shard_map/ppermute | solution.py:62
  66.0 2.2 %collective-permute-start.2 = (bf16[512,640]{1,0:T(8,128)(2,1)S(1)}, bf16[512,640]{1,0:T(8,128)(2,1)S(1)}, u32[]{:S(2)}, u32[]{:S(2)}) collective-permute-start(bf16[512,640]{1,0:T(8,128)(2,1)S(1)} %constant_dynamic-update-slice_fusion.refs_1_), channel_id=1, source_target_pairs={{0,256},{256,0},{1,257},{257,1},{2,258},{258,2},{3,259},{259,3},{4... | collective-permute-start | bytes 1966088 | tf_op jit(solution)/shard_map/ppermute | solution.py:62
  68.3 2.5 %collective-permute-start.3 = (bf16[512,640]{1,0:T(8,128)(2,1)S(1)}, bf16[512,640]{1,0:T(8,128)(2,1)}, u32[]{:S(2)}, u32[]{:S(2)}) collective-permute-start(bf16[512,640]{1,0:T(8,128)(2,1)S(1)} %constant_dynamic-update-slice_fusion.refs_1_), channel_id=1, source_target_pairs={{0,258},{258,0},{2,256},{256,2},{1,259},{259,1},{3,257},{257,3},{4... | collective-permute-start | bytes 1966088 | tf_op jit(solution)/shard_map/ppermute | solution.py:264
  70.7 0.0 copy-done.3
  70.8 0.1 select_reduce_fusion.1
  70.8 0.0 collective-permute-done.6
  70.8 1.9 %collective-permute-start.9 = (bf16[256,640]{1,0:T(8,128)(2,1)S(1)}, bf16[256,640]{1,0:T(8,128)(2,1)}, u32[]{:S(2)}, u32[]{:S(2)}) collective-permute-start(bf16[256,640]{1,0:T(8,128)(2,1)S(1)} %collective-permute-done.6), channel_id=1, source_target_pairs={{0,4},{4,0},{1,5},{5,1},{2,6},{6,2},{3,7},{7,3},{8,12},{12,8},{9,1... | collective-permute-start | bytes 983048 | tf_op jit(solution)/shard_map/ppermute | solution.py:62
  72.8 0.0 all-to-all-done.1
  72.8 4.4 %collective-permute-start.4 = (bf16[8,2,8,1536]{3,2,1,0:T(8,128)(2,1)S(1)}, bf16[8,2,8,1536]{3,2,1,0:T(8,128)(2,1)S(1)}, u32[]{:S(2)}, u32[]{:S(2)}) collective-permute-start(bf16[8,2,8,1536]{3,2,1,0:T(8,128)(2,1)S(1)} %all-to-all-done.1), channel_id=1, source_target_pairs={{0,1},{1,0},{2,3},{3,2},{4,5},{5,4},{6,7},{7,6},{8,9},{9,8},{10,11... | collective-permute-start | bytes 1179656 | tf_op jit(solution)/shard_map/ppermute | solution.py:62
  77.2 0.1 copy.13.refs_7_
  77.4 1.9 %collective-permute-start.7 = (bf16[512,640]{1,0:T(8,128)(2,1)S(1)}, bf16[512,640]{1,0:T(8,128)(2,1)}, u32[]{:S(2)}, u32[]{:S(2)}) collective-permute-start(bf16[512,640]{1,0:T(8,128)(2,1)S(1)} %constant_dynamic-update-slice_fusion.refs_1_), channel_id=1, source_target_pairs={{0,1},{1,0},{2,3},{3,2},{4,5},{5,4},{6,7},{7,6},{8,9},{9,8},{10,11... | collective-permute-start | bytes 1966088 | tf_op jit(solution)/shard_map/ppermute | solution.py:62
  79.3 0.6 collective-permute-done.9
  79.9 1.0 constant_dynamic-update-slice_fusion.2.refs_3_
  80.9 5.0 %collective-permute-start.10 = (bf16[512,640]{1,0:T(8,128)(2,1)S(1)}, bf16[512,640]{1,0:T(8,128)(2,1)}, u32[]{:S(2)}, u32[]{:S(2)}) collective-permute-start(bf16[512,640]{1,0:T(8,128)(2,1)S(1)} %constant_dynamic-update-slice_fusion.2.refs_3_), channel_id=1, source_target_pairs={{0,1},{1,0},{2,3},{3,2},{4,5},{5,4},{6,7},{7,6},{8,9},{9,8},{10,11... | collective-permute-start | bytes 1966088 | tf_op jit(solution)/shard_map/ppermute | solution.py:62
  85.9 0.0 collective-permute-done.4
  85.9 0.0 all-gather.3.cloned.1.call-done
  85.9 0.0 copy-start
  86.0 1.5 %copy-done = bf16[16,112,512]{2,1,0:T(8,128)(2,1)S(1)} copy-done((bf16[16,112,512]{2,1,0:T(8,128)(2,1)S(1)}, bf16[16,112,512]{2,1,0:T(8,128)(2,1)}, u32[]{:S(2)}) %copy-start) | copy-done | bytes 1835032
  87.4 0.8 shard_map.83
  88.3 0.0 collective-permute-done.2.refs_2_
  88.3 0.0 collective-permute-done.3.refs_4_
  88.3 2.2 %collective-permute-start.11 = (bf16[512,640]{1,0:T(8,128)(2,1)}, bf16[512,640]{1,0:T(8,128)(2,1)S(1)}, u32[]{:S(2)}, u32[]{:S(2)}) collective-permute-start(bf16[512,640]{1,0:T(8,128)(2,1)} %collective-permute-done.3.refs_4_), channel_id=1, source_target_pairs={{0,1},{1,0},{2,3},{3,2},{4,5},{5,4},{6,7},{7,6},{8,9},{9,8},{10,11... | collective-permute-start | bytes 1966088 | tf_op jit(solution)/shard_map/ppermute | solution.py:62
  90.5 2.1 %collective-permute-start.8 = (bf16[512,640]{1,0:T(8,128)(2,1)S(1)}, bf16[512,640]{1,0:T(8,128)(2,1)S(1)}, u32[]{:S(2)}, u32[]{:S(2)}) collective-permute-start(bf16[512,640]{1,0:T(8,128)(2,1)S(1)} %collective-permute-done.2.refs_2_), channel_id=1, source_target_pairs={{0,1},{1,0},{2,3},{3,2},{4,5},{5,4},{6,7},{7,6},{8,9},{9,8},{10,11... | collective-permute-start | bytes 1966088 | tf_op jit(solution)/shard_map/ppermute | solution.py:62
  92.6 5.0 %shard_map.84 = (f32[512,512]{1,0:T(8,128)S(1)}, f32[512,128]{1,0:T(8,128)S(1)}, f32[512,128]{1,0:T(8,128)S(1)}) custom-call(bf16[512,640]{1,0:T(8,128)(2,1)S(1)} %get-tuple-element.30.refs_0_, bf16[512,640]{1,0:T(8,128)(2,1)S(1)} %constant_dynamic-update-slice_fusion.refs_1_, bf16[512,640]{1,0:T(8,128)(2,1)S(1)} %collective-permute-done.2.refs_2_, ...), custom_call_target="tpu_custom_call" | custom-call | flops 2281701376 | bytes 2621440 | tf_op jit(solution)/shard_map/pallas_call | solution.py:214
  97.6 0.0 collective-permute-done.7.refs_1_
  97.6 0.0 collective-permute-done.10.refs_3_
  97.6 0.0 collective-permute-done.11.refs_4_
  97.6 0.0 collective-permute-done.8.refs_2_
  97.7 6.0 %shard_map.85 = bf16[256,256]{1,0:T(8,128)(2,1)} custom-call(bf16[512,640]{1,0:T(8,128)(2,1)S(1)} %get-tuple-element.30.refs_0_, bf16[512,640]{1,0:T(8,128)(2,1)} %collective-permute-done.7.refs_1_, bf16[512,640]{1,0:T(8,128)(2,1)S(1)} %collective-permute-done.8.refs_2_, bf16[512,640]{1,0:T(8,128)(2,1)} %collective-permute-done.10.refs_3_, ...), custom_call_target="tpu_custom_call" | custom-call | flops 2281701376 | bytes 2621440 | tf_op jit(solution)/shard_map/pallas_call | solution.py:225
  (15 shorter events, 0.2 us)
Async XLA Ops:
  6.5 31.0 %copy-start.1 = (bf16[8,1536]{1,0:T(8,128)(2,1)S(1)}, bf16[8,1536]{1,0:T(8,128)(2,1)}, u32[]{:S(2)}) copy-start(bf16[8,1536]{1,0:T(8,128)(2,1)} %param.8) | copy-start | bytes 73732
  6.5 30.7 %copy-start.2 = (s32[2,32]{1,0:T(2,128)S(1)}, s32[2,32]{1,0:T(2,128)}, u32[]{:S(2)}) copy-start(s32[2,32]{1,0:T(2,128)} %param.15) | copy-start | bytes 772
  8.2 29.3 %collective-permute-start = (bf16[8,1536]{1,0:T(8,128)(2,1)}, bf16[8,1536]{1,0:T(8,128)(2,1)S(1)}, u32[]{:S(2)}, u32[]{:S(2)}) collective-permute-start(bf16[8,1536]{1,0:T(8,128)(2,1)} %param.8), channel_id=1, source_target_pairs={{0,2},{2,0},{1,3},{3,1},{4,6},{6,4},{5,7},{7,5},{8,10},{10,8},{9,1... | collective-permute-start | bytes 73736 | tf_op jit(solution)/shard_map/ppermute | solution.py:62
  13.7 29.4 %all-to-all-start = ((bf16[32,8,640]{2,1,0:T(8,128)(2,1)}), bf16[32,8,640]{2,1,0:T(8,128)(2,1)S(1)}, u32[]{:S(2)}, u32[]{:S(2)}) async-start(bf16[32,8,640]{2,1,0:T(8,128)(2,1)} %get-tuple-element.25), calls=%async_computation | async-start | bytes 655360 | tf_op jit(solution)/shard_map/all_to_all | solution.py:253
  29.4 56.6 %all-gather.3.cloned.1.call-start = ((), (), s32[]{:S(2)}) async-start(), calls=%async_computation.2 | async-start | bytes 2064384 | tf_op jit(solution)/shard_map/all_gather | solution.py:254
  29.4 6.0 %collective-permute-start.5 = (bf16[112,512]{1,0:T(8,128)(2,1)}, bf16[112,512]{1,0:T(8,128)(2,1)S(1)}, u32[]{:S(2)}, u32[]{:S(2)}) collective-permute-start(bf16[112,512]{1,0:T(8,128)(2,1)} %get-tuple-element.28), channel_id=1, source_target_pairs={{0,256},{256,0},{1,257},{257,1},{2,258},{258,2},{3,259},{259,3},{4... | collective-permute-start | bytes 344072 | tf_op jit(solution)/shard_map/ppermute | solution.py:62
  37.1 33.6 %copy-start.3 = (s32[24]{0:T(128)S(1)}, s32[24]{0:T(128)}, u32[]{:S(2)}) copy-start(s32[24]{0:T(128)} %param.14) | copy-start | bytes 292
  43.8 29.0 %all-to-all-start.1 = ((bf16[8,2,8,1536]{3,2,1,0:T(8,128)(2,1)}), bf16[8,2,8,1536]{3,2,1,0:T(8,128)(2,1)S(1)}, u32[]{:S(2)}, u32[]{:S(2)}) async-start(bf16[8,2,8,1536]{3,2,1,0:T(8,128)(2,1)} %broadcast_in_dim.70), calls=%async_computation.1 | async-start | bytes 786432 | tf_op jit(solution)/shard_map/all_to_all | solution.py:72
  49.1 16.9 %collective-permute-start.1 = (bf16[256,640]{1,0:T(8,128)(2,1)S(1)}, bf16[256,640]{1,0:T(8,128)(2,1)S(1)}, u32[]{:S(2)}, u32[]{:S(2)}) collective-permute-start(bf16[256,640]{1,0:T(8,128)(2,1)S(1)} %bitcast.17), channel_id=1, source_target_pairs={{0,4},{4,0},{1,5},{5,1},{2,6},{6,2},{3,7},{7,3},{8,12},{12,8},{9,1... | collective-permute-start | bytes 983048 | tf_op jit(solution)/shard_map/ppermute | solution.py:62
  52.5 18.3 %collective-permute-start.6 = (bf16[256,640]{1,0:T(8,128)(2,1)S(1)}, bf16[256,640]{1,0:T(8,128)(2,1)S(1)}, u32[]{:S(2)}, u32[]{:S(2)}) collective-permute-start(bf16[256,640]{1,0:T(8,128)(2,1)S(1)} %bitcast.18), channel_id=1, source_target_pairs={{0,2},{2,0},{1,3},{3,1},{4,6},{6,4},{5,7},{7,5},{8,10},{10,8},{9,1... | collective-permute-start | bytes 983048 | tf_op jit(solution)/shard_map/ppermute | solution.py:62
  66.0 22.2 %collective-permute-start.2 = (bf16[512,640]{1,0:T(8,128)(2,1)S(1)}, bf16[512,640]{1,0:T(8,128)(2,1)S(1)}, u32[]{:S(2)}, u32[]{:S(2)}) collective-permute-start(bf16[512,640]{1,0:T(8,128)(2,1)S(1)} %constant_dynamic-update-slice_fusion.refs_1_), channel_id=1, source_target_pairs={{0,256},{256,0},{1,257},{257,1},{2,258},{258,2},{3,259},{259,3},{4... | collective-permute-start | bytes 1966088 | tf_op jit(solution)/shard_map/ppermute | solution.py:62
  68.3 20.0 %collective-permute-start.3 = (bf16[512,640]{1,0:T(8,128)(2,1)S(1)}, bf16[512,640]{1,0:T(8,128)(2,1)}, u32[]{:S(2)}, u32[]{:S(2)}) collective-permute-start(bf16[512,640]{1,0:T(8,128)(2,1)S(1)} %constant_dynamic-update-slice_fusion.refs_1_), channel_id=1, source_target_pairs={{0,258},{258,0},{2,256},{256,2},{1,259},{259,1},{3,257},{257,3},{4... | collective-permute-start | bytes 1966088 | tf_op jit(solution)/shard_map/ppermute | solution.py:264
  70.8 9.0 %collective-permute-start.9 = (bf16[256,640]{1,0:T(8,128)(2,1)S(1)}, bf16[256,640]{1,0:T(8,128)(2,1)}, u32[]{:S(2)}, u32[]{:S(2)}) collective-permute-start(bf16[256,640]{1,0:T(8,128)(2,1)S(1)} %collective-permute-done.6), channel_id=1, source_target_pairs={{0,4},{4,0},{1,5},{5,1},{2,6},{6,2},{3,7},{7,3},{8,12},{12,8},{9,1... | collective-permute-start | bytes 983048 | tf_op jit(solution)/shard_map/ppermute | solution.py:62
  72.8 13.1 %collective-permute-start.4 = (bf16[8,2,8,1536]{3,2,1,0:T(8,128)(2,1)S(1)}, bf16[8,2,8,1536]{3,2,1,0:T(8,128)(2,1)S(1)}, u32[]{:S(2)}, u32[]{:S(2)}) collective-permute-start(bf16[8,2,8,1536]{3,2,1,0:T(8,128)(2,1)S(1)} %all-to-all-done.1), channel_id=1, source_target_pairs={{0,1},{1,0},{2,3},{3,2},{4,5},{5,4},{6,7},{7,6},{8,9},{9,8},{10,11... | collective-permute-start | bytes 1179656 | tf_op jit(solution)/shard_map/ppermute | solution.py:62
  77.4 20.3 %collective-permute-start.7 = (bf16[512,640]{1,0:T(8,128)(2,1)S(1)}, bf16[512,640]{1,0:T(8,128)(2,1)}, u32[]{:S(2)}, u32[]{:S(2)}) collective-permute-start(bf16[512,640]{1,0:T(8,128)(2,1)S(1)} %constant_dynamic-update-slice_fusion.refs_1_), channel_id=1, source_target_pairs={{0,1},{1,0},{2,3},{3,2},{4,5},{5,4},{6,7},{7,6},{8,9},{9,8},{10,11... | collective-permute-start | bytes 1966088 | tf_op jit(solution)/shard_map/ppermute | solution.py:62
  80.9 16.7 %collective-permute-start.10 = (bf16[512,640]{1,0:T(8,128)(2,1)S(1)}, bf16[512,640]{1,0:T(8,128)(2,1)}, u32[]{:S(2)}, u32[]{:S(2)}) collective-permute-start(bf16[512,640]{1,0:T(8,128)(2,1)S(1)} %constant_dynamic-update-slice_fusion.2.refs_3_), channel_id=1, source_target_pairs={{0,1},{1,0},{2,3},{3,2},{4,5},{5,4},{6,7},{7,6},{8,9},{9,8},{10,11... | collective-permute-start | bytes 1966088 | tf_op jit(solution)/shard_map/ppermute | solution.py:62
  85.9 1.5 %copy-start = (bf16[16,112,512]{2,1,0:T(8,128)(2,1)S(1)}, bf16[16,112,512]{2,1,0:T(8,128)(2,1)}, u32[]{:S(2)}) copy-start(bf16[16,112,512]{2,1,0:T(8,128)(2,1)} %all-gather.3.cloned.1.call-done) | copy-start | bytes 5505028
  88.3 9.4 %collective-permute-start.11 = (bf16[512,640]{1,0:T(8,128)(2,1)}, bf16[512,640]{1,0:T(8,128)(2,1)S(1)}, u32[]{:S(2)}, u32[]{:S(2)}) collective-permute-start(bf16[512,640]{1,0:T(8,128)(2,1)} %collective-permute-done.3.refs_4_), channel_id=1, source_target_pairs={{0,1},{1,0},{2,3},{3,2},{4,5},{5,4},{6,7},{7,6},{8,9},{9,8},{10,11... | collective-permute-start | bytes 1966088 | tf_op jit(solution)/shard_map/ppermute | solution.py:62
  90.5 7.1 %collective-permute-start.8 = (bf16[512,640]{1,0:T(8,128)(2,1)S(1)}, bf16[512,640]{1,0:T(8,128)(2,1)S(1)}, u32[]{:S(2)}, u32[]{:S(2)}) collective-permute-start(bf16[512,640]{1,0:T(8,128)(2,1)S(1)} %collective-permute-done.2.refs_2_), channel_id=1, source_target_pairs={{0,1},{1,0},{2,3},{3,2},{4,5},{5,4},{6,7},{7,6},{8,9},{9,8},{10,11... | collective-permute-start | bytes 1966088 | tf_op jit(solution)/shard_map/ppermute | solution.py:62
Sparse Core Ops, SparseCore 0:
  37.2 40.5 all-gather.2

commit v3 on v2

--- a/solution.py
+++ b/solution.py
@@ -268,7 +268,6 @@
 
     query, value_up = project(core, q_half.reshape(128, 1536), q_core.reshape(128, 1536), weights)
 
-    x1_pair, x3_pair, query = lax.optimization_barrier((x1_pair, x3_pair, query))
     mine = [pair, x1_pair, x2_pair, x3_pair]
     theirs = [swap(piece, "c") for piece in mine]
 

time: 111 us -> 103 us (0.928)
  waiting for transfers between devices: 20.8 us -> 9.06 us
  starting transfers between devices: 56.4 us -> 59.5 us
    ppermute x11, waiting for transfers between devices: 15.3 us -> 3.25 us  [swap(): return lax.ppermute(x, axis, [(0, 1), (1, 0)])]
    ppermute x1, starting transfers between devices: 2.47 us -> 4.39 us  [body(): x3_pair = lax.ppermute(pair, ('xl', 'xh'), [(0, 3), (3, 0), (1, 2), (2, 1)])]
  transfers between devices with their start and end apart: 15 -> 15, of which waited for: 4 -> 3; matrix products, arithmetic and copies ran while one was open for 4% -> 4% of each run, Pallas kernels for 5% -> 6%
where the time goes in v3:
time: 103 us; the launch traced here: 102 us
  starting transfers between devices  59.5 us (58%)
  Pallas kernels  13.9 us (13%)
  between operations  13.8 us (13%)
  waiting for transfers between devices  9.06 us (9%)
  other arithmetic  2.96 us (3%)
  local copies, waits for them, and re-layouts  2.79 us (3%)
    ppermute x11, starting transfers between devices, swap(): return lax.ppermute(x, axis, [(0, 1), (1, 0)])  33 us
    all_to_all x1, starting transfers between devices, body(): near = lax.all_to_all(kv, (*Z, 'y2'), 0, 0).reshape(256, WIDTH)  15.7 us
    pallas_call x1, Pallas kernels, attention(): pl.pallas_call(second_half_kernel, out_shape=jax.ShapeDtypeStruct((rows /...  6.44 us
    all_to_all x1, starting transfers between devices, gather_direct(): lax.all_to_all(jnp.broadcast_to(x[None], (members,) + x.shape), axes, 0, 0)  6.39 us
    all_to_all x1, waiting for transfers between devices, body(): near = lax.all_to_all(kv, (*Z, 'y2'), 0, 0).reshape(256, WIDTH)  5.78 us
    pallas_call x1, Pallas kernels, attention(): pl.pallas_call(first_half_kernel, out_shape=(jax.ShapeDtypeStruct((rows,...  4.96 us
    ppermute x1, starting transfers between devices, body(): x3_pair = lax.ppermute(pair, ('xl', 'xh'), [(0, 3), (3, 0), (1, 2), (2, 1)])  4.39 us
    ppermute x11, waiting for transfers between devices, swap(): return lax.ppermute(x, axis, [(0, 1), (1, 0)])  3.25 us
  transfers between devices with their start and end apart: 15, of which 3 were waited for; matrix products, arithmetic and copies ran while one was open for 4% of the time, Pallas kernels for 6%

profile of v3, /device:TPU:1, one launch (start us, length us, event | category | flops | bytes accessed | tf_op | source)
XLA Modules:
  0.0 102.0 jit_solution(12961099462134924595)
XLA Ops:
  6.5 0.0 copy-start.1
  6.5 1.7 %shard_map.82 = (bf16[32,8,640]{2,1,0:T(8,128)(2,1)}, bf16[112,512]{1,0:T(8,128)(2,1)}) custom-call(bf16[8,576]{1,0:T(8,128)(2,1)} %kv_ref.1, bf16[96,256]{1,0:T(8,128)(2,1)} %wp_ref.1, bf16[96,128]{1,0:T(8,128)(2,1)} %wr_ref.1, bf16[32,256]{1,0:T(8,128)(2,1)} %ku_ref.1, bf16[32,256]{1,0:T(8,128)(2,1)} %vu_ref.1), custom_call_target="tpu_custom_call" | custom-call | tf_op jit(solution)/shard_map/pallas_call | solution.py:50
  8.2 5.5 %collective-permute-start = (bf16[8,1536]{1,0:T(8,128)(2,1)}, bf16[8,1536]{1,0:T(8,128)(2,1)S(1)}, u32[]{:S(2)}, u32[]{:S(2)}) collective-permute-start(bf16[8,1536]{1,0:T(8,128)(2,1)} %param.8), channel_id=1, source_target_pairs={{0,2},{2,0},{1,3},{3,1},{4,6},{6,4},{5,7},{7,5},{8,10},{10,8},{9,1... | collective-permute-start | bytes 73736 | tf_op jit(solution)/shard_map/ppermute | solution.py:62
  13.7 15.7 %all-to-all-start = ((bf16[32,8,640]{2,1,0:T(8,128)(2,1)}), bf16[32,8,640]{2,1,0:T(8,128)(2,1)S(1)}, u32[]{:S(2)}, u32[]{:S(2)}) async-start(bf16[32,8,640]{2,1,0:T(8,128)(2,1)} %get-tuple-element.22), calls=%async_computation | async-start | bytes 655360 | tf_op jit(solution)/shard_map/all_to_all | solution.py:253
  29.4 0.0 all-gather.3.cloned.1.call-start
  29.4 2.2 %collective-permute-start.2 = (bf16[112,512]{1,0:T(8,128)(2,1)}, bf16[112,512]{1,0:T(8,128)(2,1)S(1)}, u32[]{:S(2)}, u32[]{:S(2)}) collective-permute-start(bf16[112,512]{1,0:T(8,128)(2,1)} %get-tuple-element.24), channel_id=1, source_target_pairs={{0,256},{256,0},{1,257},{257,1},{2,258},{258,2},{3,259},{259,3},{4... | collective-permute-start | bytes 344072 | tf_op jit(solution)/shard_map/ppermute | solution.py:62
  31.7 0.1 add_add_fusion
  31.8 0.2 reshape.345
  32.1 0.1 iota_compare_fusion
  32.2 0.9 select_reduce_fusion
  33.1 2.4 %collective-permute-done.2 = bf16[112,512]{1,0:T(8,128)(2,1)S(1)} collective-permute-done((bf16[112,512]{1,0:T(8,128)(2,1)}, bf16[112,512]{1,0:T(8,128)(2,1)S(1)}, u32[]{:S(2)}, u32[]{:S(2)}) %collective-permute-start.2) | collective-permute-done | bytes 114720 | tf_op jit(solution)/shard_map/ppermute | solution.py:62
  35.5 0.9 select_bitcast_fusion.1
  36.4 0.0 copy-start.2
  36.4 0.7 pad_maximum_fusion
  37.1 0.0 all-gather.3.cloned.1.call-update
  37.2 0.0 collective-permute-done
  37.2 0.0 copy-done.1
  37.3 5.8 %all-to-all-done = bf16[32,8,640]{2,1,0:T(8,128)(2,1)S(1)} async-done(((bf16[32,8,640]{2,1,0:T(8,128)(2,1)}), bf16[32,8,640]{2,1,0:T(8,128)(2,1)S(1)}, u32[]{:S(2)}, u32[]{:S(2)}) %all-to-all-start) | async-done | bytes 327712 | tf_op jit(solution)/shard_map/all_to_all | solution.py:253
  43.0 1.9 %collective-permute-start.4 = (bf16[256,640]{1,0:T(8,128)(2,1)S(1)}, bf16[256,640]{1,0:T(8,128)(2,1)S(1)}, u32[]{:S(2)}, u32[]{:S(2)}) collective-permute-start(bf16[256,640]{1,0:T(8,128)(2,1)S(1)} %bitcast.17), channel_id=1, source_target_pairs={{0,4},{4,0},{1,5},{5,1},{2,6},{6,2},{3,7},{7,3},{8,12},{12,8},{9,1... | collective-permute-start | bytes 983048 | tf_op jit(solution)/shard_map/ppermute | solution.py:62
  45.0 2.1 %collective-permute-start.3 = (bf16[256,640]{1,0:T(8,128)(2,1)S(1)}, bf16[256,640]{1,0:T(8,128)(2,1)S(1)}, u32[]{:S(2)}, u32[]{:S(2)}) collective-permute-start(bf16[256,640]{1,0:T(8,128)(2,1)S(1)} %bitcast.18), channel_id=1, source_target_pairs={{0,2},{2,0},{1,3},{3,1},{4,6},{6,4},{5,7},{7,5},{8,10},{10,8},{9,1... | collective-permute-start | bytes 983048 | tf_op jit(solution)/shard_map/ppermute | solution.py:62
  47.1 0.8 broadcast_in_dim.70
  47.9 6.4 %all-to-all-start.1 = ((bf16[8,2,8,1536]{3,2,1,0:T(8,128)(2,1)}), bf16[8,2,8,1536]{3,2,1,0:T(8,128)(2,1)S(1)}, u32[]{:S(2)}, u32[]{:S(2)}) async-start(bf16[8,2,8,1536]{3,2,1,0:T(8,128)(2,1)} %broadcast_in_dim.70), calls=%async_computation.1 | async-start | bytes 786432 | tf_op jit(solution)/shard_map/all_to_all | solution.py:72
  54.3 0.0 collective-permute-done.4
  54.4 4.4 %collective-permute-start.10 = (bf16[512,640]{1,0:T(8,128)(2,1)S(1)}, bf16[512,640]{1,0:T(8,128)(2,1)S(1)}, u32[]{:S(2)}, u32[]{:S(2)}) collective-permute-start(bf16[512,640]{1,0:T(8,128)(2,1)S(1)} %constant_dynamic-update-slice_fusion.refs_1_), channel_id=1, source_target_pairs={{0,258},{258,0},{2,256},{256,2},{1,259},{259,1},{3,257},{257,3},{4... | collective-permute-start | bytes 1966088 | tf_op jit(solution)/shard_map/ppermute | solution.py:264
  58.8 1.9 %collective-permute-start.6 = (bf16[512,640]{1,0:T(8,128)(2,1)S(1)}, bf16[512,640]{1,0:T(8,128)(2,1)}, u32[]{:S(2)}, u32[]{:S(2)}) collective-permute-start(bf16[512,640]{1,0:T(8,128)(2,1)S(1)} %constant_dynamic-update-slice_fusion.refs_1_), channel_id=1, source_target_pairs={{0,256},{256,0},{1,257},{257,1},{2,258},{258,2},{3,259},{259,3},{4... | collective-permute-start | bytes 1966088 | tf_op jit(solution)/shard_map/ppermute | solution.py:62
  60.7 0.0 copy-done.2
  60.7 0.1 select_reduce_fusion.1
  60.8 0.0 collective-permute-done.3
  60.8 3.4 %collective-permute-start.8 = (bf16[256,640]{1,0:T(8,128)(2,1)S(1)}, bf16[256,640]{1,0:T(8,128)(2,1)S(1)}, u32[]{:S(2)}, u32[]{:S(2)}) collective-permute-start(bf16[256,640]{1,0:T(8,128)(2,1)S(1)} %collective-permute-done.3), channel_id=1, source_target_pairs={{0,4},{4,0},{1,5},{5,1},{2,6},{6,2},{3,7},{7,3},{8,12},{12,8},{9,1... | collective-permute-start | bytes 983048 | tf_op jit(solution)/shard_map/ppermute | solution.py:62
  64.2 0.1 copy.13.refs_7_
  64.4 4.9 %collective-permute-start.5 = (bf16[512,640]{1,0:T(8,128)(2,1)S(1)}, bf16[512,640]{1,0:T(8,128)(2,1)}, u32[]{:S(2)}, u32[]{:S(2)}) collective-permute-start(bf16[512,640]{1,0:T(8,128)(2,1)S(1)} %constant_dynamic-update-slice_fusion.refs_1_), channel_id=1, source_target_pairs={{0,1},{1,0},{2,3},{3,2},{4,5},{5,4},{6,7},{7,6},{8,9},{9,8},{10,11... | collective-permute-start | bytes 1966088 | tf_op jit(solution)/shard_map/ppermute | solution.py:62
  69.3 0.9 collective-permute-done.8
  70.2 4.9 %collective-permute-start.9 = (bf16[512,640]{1,0:T(8,128)(2,1)S(1)}, bf16[512,640]{1,0:T(8,128)(2,1)}, u32[]{:S(2)}, u32[]{:S(2)}) collective-permute-start(bf16[512,640]{1,0:T(8,128)(2,1)S(1)} %constant_dynamic-update-slice_fusion.2.refs_3_), channel_id=1, source_target_pairs={{0,1},{1,0},{2,3},{3,2},{4,5},{5,4},{6,7},{7,6},{8,9},{9,8},{10,11... | collective-permute-start | bytes 1966088 | tf_op jit(solution)/shard_map/ppermute | solution.py:62
  75.1 0.0 all-to-all-done.1
  75.1 1.9 %collective-permute-start.1 = (bf16[8,2,8,1536]{3,2,1,0:T(8,128)(2,1)S(1)}, bf16[8,2,8,1536]{3,2,1,0:T(8,128)(2,1)S(1)}, u32[]{:S(2)}, u32[]{:S(2)}) collective-permute-start(bf16[8,2,8,1536]{3,2,1,0:T(8,128)(2,1)S(1)} %all-to-all-done.1), channel_id=1, source_target_pairs={{0,1},{1,0},{2,3},{3,2},{4,5},{5,4},{6,7},{7,6},{8,9},{9,8},{10,11... | collective-permute-start | bytes 1179656 | tf_op jit(solution)/shard_map/ppermute | solution.py:62
  77.0 0.0 collective-permute-done.10.refs_4_
  77.0 2.4 %collective-permute-start.11 = (bf16[512,640]{1,0:T(8,128)(2,1)S(1)}, bf16[512,640]{1,0:T(8,128)(2,1)}, u32[]{:S(2)}, u32[]{:S(2)}) collective-permute-start(bf16[512,640]{1,0:T(8,128)(2,1)S(1)} %collective-permute-done.10.refs_4_), channel_id=1, source_target_pairs={{0,1},{1,0},{2,3},{3,2},{4,5},{5,4},{6,7},{7,6},{8,9},{9,8},{10,11... | collective-permute-start | bytes 1966088 | tf_op jit(solution)/shard_map/ppermute | solution.py:62
  79.4 0.0 collective-permute-done.6.refs_2_
  79.4 1.9 %collective-permute-start.7 = (bf16[512,640]{1,0:T(8,128)(2,1)}, bf16[512,640]{1,0:T(8,128)(2,1)}, u32[]{:S(2)}, u32[]{:S(2)}) collective-permute-start(bf16[512,640]{1,0:T(8,128)(2,1)} %collective-permute-done.6.refs_2_), channel_id=1, source_target_pairs={{0,1},{1,0},{2,3},{3,2},{4,5},{5,4},{6,7},{7,6},{8,9},{9,8},{10,11... | collective-permute-start | bytes 1966088 | tf_op jit(solution)/shard_map/ppermute | solution.py:62
  81.4 0.0 collective-permute-done.1
  81.4 0.0 all-gather.3.cloned.1.call-done
  81.4 0.0 copy-start
  81.4 1.5 %copy-done = bf16[16,112,512]{2,1,0:T(8,128)(2,1)S(1)} copy-done((bf16[16,112,512]{2,1,0:T(8,128)(2,1)S(1)}, bf16[16,112,512]{2,1,0:T(8,128)(2,1)}, u32[]{:S(2)}) %copy-start) | copy-done | bytes 1835032
  82.9 0.8 shard_map.83
  83.7 5.0 %shard_map.84 = (f32[512,512]{1,0:T(8,128)S(1)}, f32[512,128]{1,0:T(8,128)S(1)}, f32[512,128]{1,0:T(8,128)S(1)}) custom-call(bf16[512,640]{1,0:T(8,128)(2,1)S(1)} %get-tuple-element.25.refs_0_, bf16[512,640]{1,0:T(8,128)(2,1)S(1)} %constant_dynamic-update-slice_fusion.refs_1_, bf16[512,640]{1,0:T(8,128)(2,1)} %collective-permute-done.6.refs_2_, ...), custom_call_target="tpu_custom_call" | custom-call | flops 2281701376 | bytes 2621440 | tf_op jit(solution)/shard_map/pallas_call | solution.py:214
  88.7 0.0 collective-permute-done.5.refs_1_
  88.7 0.0 collective-permute-done.9.refs_3_
  88.7 0.0 collective-permute-done.11.refs_4_
  88.7 0.0 collective-permute-done.7.refs_2_
  88.7 6.4 %shard_map.85 = bf16[256,256]{1,0:T(8,128)(2,1)} custom-call(bf16[512,640]{1,0:T(8,128)(2,1)S(1)} %get-tuple-element.25.refs_0_, bf16[512,640]{1,0:T(8,128)(2,1)} %collective-permute-done.5.refs_1_, bf16[512,640]{1,0:T(8,128)(2,1)} %collective-permute-done.7.refs_2_, bf16[512,640]{1,0:T(8,128)(2,1)} %collective-permute-done.9.refs_3_, ...), custom_call_target="tpu_custom_call" | custom-call | flops 2281701376 | bytes 2621440 | tf_op jit(solution)/shard_map/pallas_call | solution.py:225
  (16 shorter events, 0.3 us)
Async XLA Ops:
  6.5 30.7 %copy-start.1 = (bf16[8,1536]{1,0:T(8,128)(2,1)S(1)}, bf16[8,1536]{1,0:T(8,128)(2,1)}, u32[]{:S(2)}) copy-start(bf16[8,1536]{1,0:T(8,128)(2,1)} %param.8) | copy-start | bytes 73732
  8.2 29.0 %collective-permute-start = (bf16[8,1536]{1,0:T(8,128)(2,1)}, bf16[8,1536]{1,0:T(8,128)(2,1)S(1)}, u32[]{:S(2)}, u32[]{:S(2)}) collective-permute-start(bf16[8,1536]{1,0:T(8,128)(2,1)} %param.8), channel_id=1, source_target_pairs={{0,2},{2,0},{1,3},{3,1},{4,6},{6,4},{5,7},{7,5},{8,10},{10,8},{9,1... | collective-permute-start | bytes 73736 | tf_op jit(solution)/shard_map/ppermute | solution.py:62
  13.7 29.4 %all-to-all-start = ((bf16[32,8,640]{2,1,0:T(8,128)(2,1)}), bf16[32,8,640]{2,1,0:T(8,128)(2,1)S(1)}, u32[]{:S(2)}, u32[]{:S(2)}) async-start(bf16[32,8,640]{2,1,0:T(8,128)(2,1)} %get-tuple-element.22), calls=%async_computation | async-start | bytes 655360 | tf_op jit(solution)/shard_map/all_to_all | solution.py:253
  29.4 52.0 %all-gather.3.cloned.1.call-start = ((), (), s32[]{:S(2)}) async-start(), calls=%async_computation.2 | async-start | bytes 2064384 | tf_op jit(solution)/shard_map/all_gather | solution.py:254
  29.4 6.0 %collective-permute-start.2 = (bf16[112,512]{1,0:T(8,128)(2,1)}, bf16[112,512]{1,0:T(8,128)(2,1)S(1)}, u32[]{:S(2)}, u32[]{:S(2)}) collective-permute-start(bf16[112,512]{1,0:T(8,128)(2,1)} %get-tuple-element.24), channel_id=1, source_target_pairs={{0,256},{256,0},{1,257},{257,1},{2,258},{258,2},{3,259},{259,3},{4... | collective-permute-start | bytes 344072 | tf_op jit(solution)/shard_map/ppermute | solution.py:62
  36.4 24.3 %copy-start.2 = (s32[24]{0:T(128)S(1)}, s32[24]{0:T(128)}, u32[]{:S(2)}) copy-start(s32[24]{0:T(128)} %param.14) | copy-start | bytes 292
  43.0 11.3 %collective-permute-start.4 = (bf16[256,640]{1,0:T(8,128)(2,1)S(1)}, bf16[256,640]{1,0:T(8,128)(2,1)S(1)}, u32[]{:S(2)}, u32[]{:S(2)}) collective-permute-start(bf16[256,640]{1,0:T(8,128)(2,1)S(1)} %bitcast.17), channel_id=1, source_target_pairs={{0,4},{4,0},{1,5},{5,1},{2,6},{6,2},{3,7},{7,3},{8,12},{12,8},{9,1... | collective-permute-start | bytes 983048 | tf_op jit(solution)/shard_map/ppermute | solution.py:62
  45.0 15.8 %collective-permute-start.3 = (bf16[256,640]{1,0:T(8,128)(2,1)S(1)}, bf16[256,640]{1,0:T(8,128)(2,1)S(1)}, u32[]{:S(2)}, u32[]{:S(2)}) collective-permute-start(bf16[256,640]{1,0:T(8,128)(2,1)S(1)} %bitcast.18), channel_id=1, source_target_pairs={{0,2},{2,0},{1,3},{3,1},{4,6},{6,4},{5,7},{7,5},{8,10},{10,8},{9,1... | collective-permute-start | bytes 983048 | tf_op jit(solution)/shard_map/ppermute | solution.py:62
  47.9 27.2 %all-to-all-start.1 = ((bf16[8,2,8,1536]{3,2,1,0:T(8,128)(2,1)}), bf16[8,2,8,1536]{3,2,1,0:T(8,128)(2,1)S(1)}, u32[]{:S(2)}, u32[]{:S(2)}) async-start(bf16[8,2,8,1536]{3,2,1,0:T(8,128)(2,1)} %broadcast_in_dim.70), calls=%async_computation.1 | async-start | bytes 786432 | tf_op jit(solution)/shard_map/all_to_all | solution.py:72
  54.4 22.6 %collective-permute-start.10 = (bf16[512,640]{1,0:T(8,128)(2,1)S(1)}, bf16[512,640]{1,0:T(8,128)(2,1)S(1)}, u32[]{:S(2)}, u32[]{:S(2)}) collective-permute-start(bf16[512,640]{1,0:T(8,128)(2,1)S(1)} %constant_dynamic-update-slice_fusion.refs_1_), channel_id=1, source_target_pairs={{0,258},{258,0},{2,256},{256,2},{1,259},{259,1},{3,257},{257,3},{4... | collective-permute-start | bytes 1966088 | tf_op jit(solution)/shard_map/ppermute | solution.py:264
  58.8 20.7 %collective-permute-start.6 = (bf16[512,640]{1,0:T(8,128)(2,1)S(1)}, bf16[512,640]{1,0:T(8,128)(2,1)}, u32[]{:S(2)}, u32[]{:S(2)}) collective-permute-start(bf16[512,640]{1,0:T(8,128)(2,1)S(1)} %constant_dynamic-update-slice_fusion.refs_1_), channel_id=1, source_target_pairs={{0,256},{256,0},{1,257},{257,1},{2,258},{258,2},{3,259},{259,3},{4... | collective-permute-start | bytes 1966088 | tf_op jit(solution)/shard_map/ppermute | solution.py:62
  60.8 9.3 %collective-permute-start.8 = (bf16[256,640]{1,0:T(8,128)(2,1)S(1)}, bf16[256,640]{1,0:T(8,128)(2,1)S(1)}, u32[]{:S(2)}, u32[]{:S(2)}) collective-permute-start(bf16[256,640]{1,0:T(8,128)(2,1)S(1)} %collective-permute-done.3), channel_id=1, source_target_pairs={{0,4},{4,0},{1,5},{5,1},{2,6},{6,2},{3,7},{7,3},{8,12},{12,8},{9,1... | collective-permute-start | bytes 983048 | tf_op jit(solution)/shard_map/ppermute | solution.py:62
  64.4 24.3 %collective-permute-start.5 = (bf16[512,640]{1,0:T(8,128)(2,1)S(1)}, bf16[512,640]{1,0:T(8,128)(2,1)}, u32[]{:S(2)}, u32[]{:S(2)}) collective-permute-start(bf16[512,640]{1,0:T(8,128)(2,1)S(1)} %constant_dynamic-update-slice_fusion.refs_1_), channel_id=1, source_target_pairs={{0,1},{1,0},{2,3},{3,2},{4,5},{5,4},{6,7},{7,6},{8,9},{9,8},{10,11... | collective-permute-start | bytes 1966088 | tf_op jit(solution)/shard_map/ppermute | solution.py:62
  70.2 18.5 %collective-permute-start.9 = (bf16[512,640]{1,0:T(8,128)(2,1)S(1)}, bf16[512,640]{1,0:T(8,128)(2,1)}, u32[]{:S(2)}, u32[]{:S(2)}) collective-permute-start(bf16[512,640]{1,0:T(8,128)(2,1)S(1)} %constant_dynamic-update-slice_fusion.2.refs_3_), channel_id=1, source_target_pairs={{0,1},{1,0},{2,3},{3,2},{4,5},{5,4},{6,7},{7,6},{8,9},{9,8},{10,11... | collective-permute-start | bytes 1966088 | tf_op jit(solution)/shard_map/ppermute | solution.py:62
  75.1 6.3 %collective-permute-start.1 = (bf16[8,2,8,1536]{3,2,1,0:T(8,128)(2,1)S(1)}, bf16[8,2,8,1536]{3,2,1,0:T(8,128)(2,1)S(1)}, u32[]{:S(2)}, u32[]{:S(2)}) collective-permute-start(bf16[8,2,8,1536]{3,2,1,0:T(8,128)(2,1)S(1)} %all-to-all-done.1), channel_id=1, source_target_pairs={{0,1},{1,0},{2,3},{3,2},{4,5},{5,4},{6,7},{7,6},{8,9},{9,8},{10,11... | collective-permute-start | bytes 1179656 | tf_op jit(solution)/shard_map/ppermute | solution.py:62
  77.0 11.7 %collective-permute-start.11 = (bf16[512,640]{1,0:T(8,128)(2,1)S(1)}, bf16[512,640]{1,0:T(8,128)(2,1)}, u32[]{:S(2)}, u32[]{:S(2)}) collective-permute-start(bf16[512,640]{1,0:T(8,128)(2,1)S(1)} %collective-permute-done.10.refs_4_), channel_id=1, source_target_pairs={{0,1},{1,0},{2,3},{3,2},{4,5},{5,4},{6,7},{7,6},{8,9},{9,8},{10,11... | collective-permute-start | bytes 1966088 | tf_op jit(solution)/shard_map/ppermute | solution.py:62
  79.4 9.3 %collective-permute-start.7 = (bf16[512,640]{1,0:T(8,128)(2,1)}, bf16[512,640]{1,0:T(8,128)(2,1)}, u32[]{:S(2)}, u32[]{:S(2)}) collective-permute-start(bf16[512,640]{1,0:T(8,128)(2,1)} %collective-permute-done.6.refs_2_), channel_id=1, source_target_pairs={{0,1},{1,0},{2,3},{3,2},{4,5},{5,4},{6,7},{7,6},{8,9},{9,8},{10,11... | collective-permute-start | bytes 1966088 | tf_op jit(solution)/shard_map/ppermute | solution.py:62
  81.4 1.5 %copy-start = (bf16[16,112,512]{2,1,0:T(8,128)(2,1)S(1)}, bf16[16,112,512]{2,1,0:T(8,128)(2,1)}, u32[]{:S(2)}) copy-start(bf16[16,112,512]{2,1,0:T(8,128)(2,1)} %all-gather.3.cloned.1.call-done) | copy-start | bytes 5505028
Sparse Core Ops, SparseCore 0:
  37.3 40.2 all-gather.2

commit v4 on v3

v4 whole, which is shorter than its diff:
```python
import jax
import jax.numpy as jnp
import numpy as np
from jax import lax
from jax.experimental import pallas as pl
from jax.experimental.pallas import tpu as pltpu
from jax.sharding import Mesh, PartitionSpec as P

LATENT_WIDTH = 512
ROTARY_DIMS = 64
PLAIN_QUERY_DIMS = 128
VALUE_DIMS = 128
TILE = 128
WIDTH = 640
PROJECT_COST = 5_000_000_000
SCALE = (PLAIN_QUERY_DIMS + ROTARY_DIMS) ** (-0.5)
FACTOR = SCALE * 1.4426950408889634
NEG = -1e30
FLOOR = -1e29

AXES = ("xl", "z2", "z1", "y2", "y1", "xh", "c")
SIZES = (2, 4, 2, 4, 2, 2, 2)
Z = ("z2", "z1")
BLK = ("xl", "z2", "z1")
WIDE = ("y2", "y1", "xh", "c")


def prepare_kernel(kv_ref, wp_ref, wr_ref, ku_ref, vu_ref, kv_out, w_out):
    raw = kv_ref[...].astype(jnp.float32)
    latent = raw[:, :LATENT_WIDTH]
    energy = jnp.mean(latent * latent, axis=1, keepdims=True)
    normed = (latent * lax.rsqrt(energy + 1e-06)).astype(jnp.bfloat16)
    rope = raw[:, LATENT_WIDTH:]
    rope = jnp.concatenate([rope, jnp.zeros_like(rope)], axis=1).astype(jnp.bfloat16)
    for copy in range(kv_out.shape[0]):
        kv_out[copy, :, 0:LATENT_WIDTH] = normed
        kv_out[copy, :, LATENT_WIDTH:WIDTH] = rope
    w_out[0:96, 0:256] = wp_ref[...]
    w_out[0:96, 256:384] = wr_ref[...]
    w_out[0:32, 384:512] = ku_ref[:, 0:128]
    w_out[32:64, 384:512] = ku_ref[:, 128:256]
    w_out[64:96, 384:512] = vu_ref[:, 0:128]
    w_out[96:112, 0:128] = vu_ref[0:16, 128:256]
    w_out[96:112, 128:256] = vu_ref[16:32, 128:256]
    w_out[96:112, 256:512] = jnp.zeros((16, 256), jnp.bfloat16)


def prepare(kv_raw, wp, wr, ku, vu):
    vmem = pl.BlockSpec(memory_space=pltpu.VMEM)
    return pl.pallas_call(
        prepare_kernel,
        out_shape=(
            jax.ShapeDtypeStruct((32, 8, WIDTH), jnp.bfloat16),
            jax.ShapeDtypeStruct((112, 512), jnp.bfloat16),
        ),
        in_specs=[vmem] * 5,
        out_specs=(vmem, vmem),
    )(kv_raw, wp, wr, ku, vu)


def swap(x, axis):
    return lax.ppermute(x, axis, [(0, 1), (1, 0)])


def in_order(bit, own, other, axis):
    first = jnp.where(bit == 0, own, other)
    second = jnp.where(bit == 0, other, own)
    return jnp.concatenate([first, second], axis=axis)


def gather_direct(x, axes, members):
    return lax.all_to_all(jnp.broadcast_to(x[None], (members,) + x.shape), axes, 0, 0)


def project_kernel(place_ref, mine_ref, other_ref, w_ref, q_out, vu_out):
    x_lo = place_ref[1]
    half_at = [x_lo, 1 - x_lo]

    def rows_of(first, many, cols):
        parts = [w_ref[:, pl.ds(at, 1), first : first + many, cols] for at in half_at]
        return [part.reshape(8 * many, part.shape[-1]) for part in parts]

    low, high = rows_of(0, 96, slice(0, 384))

    def product(ref):
        return jnp.dot(ref[:, 0:768], low, preferred_element_type=jnp.float32) + jnp.dot(
            ref[:, 768:1536], high, preferred_element_type=jnp.float32
        )

    mine, other = product(mine_ref), product(other_ref)
    is_first = place_ref[0] == 0
    parts = [jnp.where(is_first, mine, other), jnp.where(is_first, other, mine)]
    projected = jnp.stack([part.reshape(16, 8, 384) for part in parts], axis=1).reshape(256, 384)
    for head in range(2):
        nope = projected[:, head * 128 : head * 128 + 128].astype(jnp.bfloat16)
        rope = projected[:, 256 + head * 64 : 320 + head * 64]
        key_up = jnp.concatenate(rows_of(32 * head, 32, slice(384, 512)), axis=0)
        absorbed = lax.dot_general(nope, key_up, (((1,), (1,)), ((), ())), preferred_element_type=jnp.float32)
        at = pl.ds(head * 256, 256)
        q_out[at, 0:LATENT_WIDTH] = absorbed.astype(jnp.bfloat16)
        q_out[at, LATENT_WIDTH:WIDTH] = jnp.concatenate([rope, jnp.zeros_like(rope)], axis=1).astype(jnp.bfloat16)
    vu_out[:, 0:128] = jnp.concatenate(rows_of(64, 32, slice(384, 512)), axis=0)
    for half in range(2):
        upper = [w_ref[:, pl.ds(half_at[half], 1), 96:112, 128 * j : 128 * j + 128] for j in range(2)]
        vu_out[pl.ds(half * 256, 256), 128:256] = jnp.concatenate(upper, axis=2).reshape(256, 128)


def project(place, mine, other, weights):
    vmem = pl.BlockSpec(memory_space=pltpu.VMEM)
    return pl.pallas_call(
        project_kernel,
        out_shape=(
            jax.ShapeDtypeStruct((4 * mine.shape[0], WIDTH), jnp.bfloat16),
            jax.ShapeDtypeStruct((LATENT_WIDTH, 2 * VALUE_DIMS), jnp.bfloat16),
        ),
        in_specs=[pl.BlockSpec(memory_space=pltpu.SMEM)] + [vmem] * 3,
        out_specs=(vmem, vmem),
        compiler_params=pltpu.CompilerParams(vmem_limit_bytes=16 * 1024 * 1024),
        cost_estimate=pl.CostEstimate(flops=PROJECT_COST, bytes_accessed=0, transcendentals=0),
    )(place, mine, other, weights)


def attention_kernel(q_ref, vu_ref, low_ref, high_ref, bounds_ref, *refs):
    pieces, (o_ref, keys_ref, s_ref, sems) = refs[:-4], refs[-4:]
    step, many = pieces[0].shape[0], len(pieces) // 2
    fetches = []
    for i, piece in enumerate(pieces):
        fetches.append(pltpu.make_async_copy(piece, keys_ref.at[pl.ds(i * step, step), :], sems.at[i]))
        fetches[-1].start()
    q = q_ref[...]
    rows = q.shape[0]
    groups = rows // TILE
    half = groups // 2
    peaks = [jnp.full((TILE, 1), FLOOR, jnp.float32) for _ in range(groups)]
    totals = [jnp.zeros((TILE, 1), jnp.float32) for _ in range(groups)]
    summed = None
    for turn in range(2):
        for fetch in fetches[turn * many : (turn + 1) * many]:
            fetch.wait()
        highest = [jnp.full((TILE, 128), FLOOR, jnp.float32) for _ in range(groups)]
        for i in range(many):
            at = pl.ds((turn * many + i) * step, step)
            scores = lax.dot_general(
                q, keys_ref[at, :], (((1,), (1,)), ((), ())), preferred_element_type=jnp.float32
            )
            for tile in range(half):
                last = bounds_ref[pl.ds(tile * TILE, TILE), 0:1]
                first = bounds_ref[pl.ds(tile * TILE, TILE), 1:2]
                allowed = (low_ref[tile : tile + 1, at] <= last) & (high_ref[tile : tile + 1, at] >= first)
                for head in range(2):
                    g = head * half + tile
                    part = jnp.where(allowed, scores[g * TILE : (g + 1) * TILE, :], NEG)
                    s_ref[pl.ds(g * TILE, TILE), pl.ds(i * step, step)] = part
                    for lane in range(0, step, 128):
                        highest[g] = jnp.maximum(highest[g], part[:, lane : lane + 128])
        old = peaks
        peaks = [jnp.maximum(p, jnp.max(h, axis=1, keepdims=True)) for p, h in zip(old, highest)]
        sums = [jnp.zeros((TILE, 128), jnp.float32) for _ in range(groups)]
        accum = jnp.zeros((rows, LATENT_WIDTH), jnp.float32)
        for i in range(many):
            parts = []
            for g in range(groups):
                weights = jnp.exp2((s_ref[pl.ds(g * TILE, TILE), pl.ds(i * step, step)] - peaks[g]) * FACTOR)
                for lane in range(0, step, 128):
                    sums[g] = sums[g] + weights[:, lane : lane + 128]
                parts.append(weights.astype(jnp.bfloat16))
            accum = accum + jnp.dot(
                jnp.concatenate(parts, axis=0),
                keys_ref[pl.ds((turn * many + i) * step, step), 0:LATENT_WIDTH],
                preferred_element_type=jnp.float32,
            )
        sums = [jnp.sum(total, axis=1, keepdims=True) for total in sums]
        if summed is None:
            totals, summed = sums, accum
        else:
            carry = [jnp.exp2((p - new) * FACTOR) for p, new in zip(old, peaks)]
            totals = [new + total * c for new, total, c in zip(sums, totals, carry)]
            summed = accum + summed * jnp.concatenate(carry, axis=0)
    latent_out = (summed * (1.0 / jnp.concatenate(totals, axis=0))).astype(jnp.bfloat16)
    for head in range(2):
        cols = pl.ds(head * VALUE_DIMS, VALUE_DIMS)
        o_ref[:, cols] = jnp.dot(
            latent_out[head * (rows // 2) : (head + 1) * (rows // 2), :],
            vu_ref[:, cols],
            preferred_element_type=jnp.float32,
        ).astype(jnp.bfloat16)


def attention(query, value_up, pieces, low, high, bounds):
    tokens, count = query.shape[0] // 2, low.shape[1]
    vmem, hbm = pl.BlockSpec(memory_space=pltpu.VMEM), pl.BlockSpec(memory_space=pltpu.HBM)
    return pl.pallas_call(
        attention_kernel,
        out_shape=jax.ShapeDtypeStruct((tokens, 2 * VALUE_DIMS), jnp.bfloat16),
        in_specs=[vmem] * 5 + [hbm] * len(pieces),
        out_specs=vmem,
        scratch_shapes=[
            pltpu.VMEM((count, WIDTH), jnp.bfloat16),
            pltpu.VMEM((2 * tokens, count // 2), jnp.float32),
            pltpu.SemaphoreType.DMA((len(pieces),)),
        ],
        compiler_params=pltpu.CompilerParams(vmem_limit_bytes=40 * 1024 * 1024),
        cost_estimate=pl.CostEstimate(
            flops=4 * tokens * count * (576 + 512),
            bytes_accessed=count * WIDTH * 2,
            transcendentals=2 * tokens * count,
        ),
    )(query, value_up, low, high, bounds, *pieces)


def body(
    q_latent,
    kv_raw,
    query_plain_weight,
    query_rotary_weight,
    key_up_weight,
    value_up_weight,
    doc_starts,
    tile_kind,
):
    xl, z2, z1 = lax.axis_index("xl"), lax.axis_index("z2"), lax.axis_index("z1")
    y1, xh, core = lax.axis_index("y1"), lax.axis_index("xh"), lax.axis_index("c")

    kv, packed = prepare(kv_raw, query_plain_weight, query_rotary_weight, key_up_weight, value_up_weight)

    kv, packed = lax.optimization_barrier((kv, packed))
    w_pair = jnp.stack([packed, swap(packed, "xl")], axis=0)

    near = lax.all_to_all(kv, (*Z, "y2"), 0, 0).reshape(256, WIDTH)
    weights = lax.all_gather(w_pair, Z)

    q_latent, _ = lax.optimization_barrier((q_latent, near))
    q_half = gather_direct(q_latent, ("y2", "y1", "xh"), 16)
    q_core = swap(q_half, "c")

    next_y = swap(near, "y1")
    x2_near = swap(near, "xh")
    pair = jnp.concatenate([near, next_y], axis=0)
    x1_pair = swap(pair, "xl")
    x3_pair = lax.ppermute(pair, ("xl", "xh"), [(0, 3), (3, 0), (1, 2), (2, 1)])
    x2_far, pair = lax.optimization_barrier((x2_near, pair))
    x2_next = swap(x2_far, "y1")
    x2_pair = jnp.concatenate([x2_near, x2_next], axis=0)

    mine = [pair, x1_pair, x2_pair, x3_pair]
    theirs = [swap(piece, "c") for piece in mine]

    shape = (2, 4, 2, 8, 4, 8)
    at = lambda d: lax.broadcasted_iota(jnp.int32, shape, d)
    far = at(1)
    k_xl, k_xh = xl ^ (far & 1), xh ^ (far >> 1)
    k_block = k_xl * 8 + at(3)
    k_y = 2 * at(4) + (y1 ^ at(2))
    k_pos = (k_block * 256 + ((k_y * 2 + k_xh) * 2 + (core ^ at(0))) * 8 + at(5)).reshape(1, 4096)
    k_tile = k_pos // TILE
    kinds = jnp.sum(
        jnp.where(
            lax.broadcasted_iota(jnp.int32, (1, 32, 4096), 1) == k_tile[:, None, :], tile_kind[:, :, None], 0
        ),
        axis=1,
    )
    big = jnp.int32(1 << 20)
    low = jnp.where(kinds == 2, k_pos, jnp.where(kinds == 1, -1, big))
    high = jnp.where(kinds == 2, k_pos, jnp.where(kinds == 1, big, -1))
    q_pos = (xl * 8 + 2 * z2 + z1) * 256 + lax.broadcasted_iota(jnp.int32, (256, 1), 0)
    q_first = jnp.max(jnp.where(doc_starts[None, :] <= q_pos, doc_starts[None, :], 0), axis=1, keepdims=True)
    bounds = jnp.concatenate([q_pos, q_first], axis=1)
    place = jnp.stack([core, xl])
    query, value_up = project(place, q_half.reshape(128, 1536), q_core.reshape(128, 1536), weights)
    return attention(query, value_up, mine + theirs, low, high, bounds)


def solution(mesh):
    fine = Mesh(np.asarray(mesh.devices).reshape(SIZES), AXES)
    return jax.shard_map(
        body,
        mesh=fine,
        in_specs=(
            P(AXES, None),
            P(AXES, None),
            P(BLK, WIDE),
            P(BLK, WIDE),
            P(BLK, WIDE),
            P(BLK, WIDE),
            P(),
            P(BLK, None),
        ),
        out_specs=P(BLK, WIDE),
        check_vma=False,
    )
```

time: 103 us -> 102 us (level)
    ppermute x11 -> x10, starting transfers between devices: 33 us -> 31 us  [swap(): return lax.ppermute(x, axis, [(0, 1), (1, 0)])]
    another operation x0 -> x2, other arithmetic: none -> 1.68 us  [the longest x1 1.61 us: body(): w_pair = jnp.stack([packed, swap(packed, 'xl')], axis=0)]
    pallas_call x3 -> x2, Pallas kernels: 12.2 us -> 11.2 us  [the longest x1 9.43 us: attention(): pl.pallas_call(attention_kernel, out_shape=jax.ShapeDtypeStruct((tokens,...]
    ppermute x11 -> x10, waiting for transfers between devices: 3.25 us -> 2.89 us  [swap(): return lax.ppermute(x, axis, [(0, 1), (1, 0)])]
  transfers between devices with their start and end apart: 15 -> 14, of which waited for: 3 -> 3; matrix products, arithmetic and copies ran while one was open for 4% -> 4% of each run, Pallas kernels for 6% -> 2%
where the time goes in v4:
time: 102 us; the launch traced here: 101 us
  starting transfers between devices  59.5 us (58%)
  between operations  13.8 us (14%)
  Pallas kernels  12.9 us (13%)
  waiting for transfers between devices  9.19 us (9%)
  local copies, waits for them, and re-layouts  3.72 us (4%)
  other arithmetic  2.35 us (2%)
    ppermute x10, starting transfers between devices, swap(): return lax.ppermute(x, axis, [(0, 1), (1, 0)])  31 us
    all_to_all x1, starting transfers between devices, body(): near = lax.all_to_all(kv, (*Z, 'y2'), 0, 0).reshape(256, WIDTH)  16.5 us
    pallas_call x1, Pallas kernels, attention(): pl.pallas_call(attention_kernel, out_shape=jax.ShapeDtypeStruct((tokens,...  9.43 us
    all_to_all x1, starting transfers between devices, gather_direct(): lax.all_to_all(jnp.broadcast_to(x[None], (members,) + x.shape), axes, 0, 0)  6.53 us
    all_to_all x1, waiting for transfers between devices, body(): near = lax.all_to_all(kv, (*Z, 'y2'), 0, 0).reshape(256, WIDTH)  5.5 us
    ppermute x1, starting transfers between devices, body(): x3_pair = lax.ppermute(pair, ('xl', 'xh'), [(0, 3), (3, 0), (1, 2), (2, 1)])  5.35 us
    ppermute x10, waiting for transfers between devices, swap(): return lax.ppermute(x, axis, [(0, 1), (1, 0)])  2.89 us
  transfers between devices with their start and end apart: 14, of which 3 were waited for; matrix products, arithmetic and copies ran while one was open for 4% of the time, Pallas kernels for 2%

profile of v4, /device:TPU:1, one launch (start us, length us, event | category | flops | bytes accessed | tf_op | source)
XLA Modules:
  0.0 101.4 jit_solution(12186926213628478731)
XLA Ops:
  6.5 0.0 copy-start.2
  6.5 0.0 copy-start.1
  6.5 1.7 %shard_map.82 = (bf16[32,8,640]{2,1,0:T(8,128)(2,1)}, bf16[112,512]{1,0:T(8,128)(2,1)}) custom-call(bf16[8,576]{1,0:T(8,128)(2,1)} %kv_ref.1, bf16[96,256]{1,0:T(8,128)(2,1)} %wp_ref.1, bf16[96,128]{1,0:T(8,128)(2,1)} %wr_ref.1, bf16[32,256]{1,0:T(8,128)(2,1)} %ku_ref.1, bf16[32,256]{1,0:T(8,128)(2,1)} %vu_ref.1), custom_call_target="tpu_custom_call" | custom-call | tf_op jit(solution)/shard_map/pallas_call | solution.py:50
  8.2 16.5 %all-to-all-start = ((bf16[32,8,640]{2,1,0:T(8,128)(2,1)}), bf16[32,8,640]{2,1,0:T(8,128)(2,1)S(1)}, u32[]{:S(2)}, u32[]{:S(2)}) async-start(bf16[32,8,640]{2,1,0:T(8,128)(2,1)} %get-tuple-element.12), calls=%async_computation | async-start | bytes 655360 | tf_op jit(solution)/shard_map/all_to_all | solution.py:229
  24.7 0.0 all-gather.3.cloned.1.call-start
  24.8 3.1 %collective-permute-start.1 = (bf16[112,512]{1,0:T(8,128)(2,1)}, bf16[112,512]{1,0:T(8,128)(2,1)S(1)}, u32[]{:S(2)}, u32[]{:S(2)}) collective-permute-start(bf16[112,512]{1,0:T(8,128)(2,1)} %get-tuple-element.14), channel_id=1, source_target_pairs={{0,256},{256,0},{1,257},{257,1},{2,258},{258,2},{3,259},{259,3},{4... | collective-permute-start | bytes 344072 | tf_op jit(solution)/shard_map/ppermute | solution.py:62
  27.9 2.9 %collective-permute-done.1 = bf16[112,512]{1,0:T(8,128)(2,1)S(1)} collective-permute-done((bf16[112,512]{1,0:T(8,128)(2,1)}, bf16[112,512]{1,0:T(8,128)(2,1)S(1)}, u32[]{:S(2)}, u32[]{:S(2)}) %collective-permute-start.1) | collective-permute-done | bytes 114720 | tf_op jit(solution)/shard_map/ppermute | solution.py:62
  30.8 1.6 %pad_maximum_fusion.1 = bf16[2,112,512]{2,1,0:T(8,128)(2,1)} fusion(bf16[1,112,512]{2,1,0:T(8,128)(2,1)S(1)} %bitcast.15, bf16[1,112,512]{2,1,0:T(8,128)(2,1)} %bitcast.14), kind=kLoop, calls=%fused_computation.4 | loop fusion | flops 114688 | bytes 458752 | tf_op jit(solution)/shard_map/stack | solution.py:227
  32.4 0.0 all-gather.3.cloned.1.call-update
  32.4 0.1 add_add_fusion
  32.6 0.2 reshape.337
  32.8 5.5 %all-to-all-done = bf16[32,8,640]{2,1,0:T(8,128)(2,1)S(1)} async-done(((bf16[32,8,640]{2,1,0:T(8,128)(2,1)}), bf16[32,8,640]{2,1,0:T(8,128)(2,1)S(1)}, u32[]{:S(2)}, u32[]{:S(2)}) %all-to-all-start) | async-done | bytes 327712 | tf_op jit(solution)/shard_map/all_to_all | solution.py:229
  38.3 1.9 %collective-permute-start.3 = (bf16[256,640]{1,0:T(8,128)(2,1)S(1)}, bf16[256,640]{1,0:T(8,128)(2,1)S(1)}, u32[]{:S(2)}, u32[]{:S(2)}) collective-permute-start(bf16[256,640]{1,0:T(8,128)(2,1)S(1)} %bitcast.11), channel_id=1, source_target_pairs={{0,4},{4,0},{1,5},{5,1},{2,6},{6,2},{3,7},{7,3},{8,12},{12,8},{9,1... | collective-permute-start | bytes 983048 | tf_op jit(solution)/shard_map/ppermute | solution.py:62
  40.2 0.1 iota_compare_fusion
  40.3 0.0 copy-done.2
  40.3 0.2 select_reduce_fusion
  40.6 0.0 copy-start.3
  40.6 4.7 %collective-permute-start.2 = (bf16[256,640]{1,0:T(8,128)(2,1)S(1)}, bf16[256,640]{1,0:T(8,128)(2,1)S(1)}, u32[]{:S(2)}, u32[]{:S(2)}) collective-permute-start(bf16[256,640]{1,0:T(8,128)(2,1)S(1)} %bitcast.12), channel_id=1, source_target_pairs={{0,2},{2,0},{1,3},{3,1},{4,6},{6,4},{5,7},{7,5},{8,10},{10,8},{9,1... | collective-permute-start | bytes 983048 | tf_op jit(solution)/shard_map/ppermute | solution.py:62
  45.2 0.0 copy-done.1
  45.3 0.8 broadcast_in_dim.66
  46.0 6.5 %all-to-all-start.1 = ((bf16[16,8,1536]{2,1,0:T(8,128)(2,1)}), bf16[16,8,1536]{2,1,0:T(8,128)(2,1)S(1)}, u32[]{:S(2)}, u32[]{:S(2)}) async-start(bf16[16,8,1536]{2,1,0:T(8,128)(2,1)} %broadcast_in_dim.66), calls=%async_computation.1 | async-start | bytes 786432 | tf_op jit(solution)/shard_map/all_to_all | solution.py:72
  52.6 0.0 collective-permute-done.3
  52.6 0.1 pad_maximum_fusion.refs_0_
  52.7 5.3 %collective-permute-start.6 = (bf16[512,640]{1,0:T(8,128)(2,1)S(1)}, bf16[512,640]{1,0:T(8,128)(2,1)S(1)}, u32[]{:S(2)}, u32[]{:S(2)}) collective-permute-start(bf16[512,640]{1,0:T(8,128)(2,1)S(1)} %pad_maximum_fusion.refs_0_), channel_id=1, source_target_pairs={{0,258},{258,0},{2,256},{256,2},{1,259},{259,1},{3,257},{257,3},{4... | collective-permute-start | bytes 1966088 | tf_op jit(solution)/shard_map/ppermute | solution.py:240
  58.0 1.9 %collective-permute-start.4 = (bf16[512,640]{1,0:T(8,128)(2,1)S(1)}, bf16[512,640]{1,0:T(8,128)(2,1)S(1)}, u32[]{:S(2)}, u32[]{:S(2)}) collective-permute-start(bf16[512,640]{1,0:T(8,128)(2,1)S(1)} %pad_maximum_fusion.refs_0_), channel_id=1, source_target_pairs={{0,256},{256,0},{1,257},{257,1},{2,258},{258,2},{3,259},{259,3},{4... | collective-permute-start | bytes 1966088 | tf_op jit(solution)/shard_map/ppermute | solution.py:62
  60.0 0.0 collective-permute-done.2
  60.0 3.1 %collective-permute-start.5 = (bf16[256,640]{1,0:T(8,128)(2,1)S(1)}, bf16[256,640]{1,0:T(8,128)(2,1)}, u32[]{:S(2)}, u32[]{:S(2)}) collective-permute-start(bf16[256,640]{1,0:T(8,128)(2,1)S(1)} %collective-permute-done.2), channel_id=1, source_target_pairs={{0,4},{4,0},{1,5},{5,1},{2,6},{6,2},{3,7},{7,3},{8,12},{12,8},{9,1... | collective-permute-start | bytes 983048 | tf_op jit(solution)/shard_map/ppermute | solution.py:62
  63.1 0.0 copy-done.3
  63.1 0.1 select_reduce_fusion.1
  63.2 4.6 %collective-permute-start.7 = (bf16[512,640]{1,0:T(8,128)(2,1)S(1)}, bf16[512,640]{1,0:T(8,128)(2,1)}, u32[]{:S(2)}, u32[]{:S(2)}) collective-permute-start(bf16[512,640]{1,0:T(8,128)(2,1)S(1)} %pad_maximum_fusion.refs_0_), channel_id=1, source_target_pairs={{0,1},{1,0},{2,3},{3,2},{4,5},{5,4},{6,7},{7,6},{8,9},{9,8},{10,11... | collective-permute-start | bytes 1966088 | tf_op jit(solution)/shard_map/ppermute | solution.py:62
  67.9 0.0 all-to-all-done.1
  67.9 3.9 %collective-permute-start = (bf16[16,8,1536]{2,1,0:T(8,128)(2,1)S(1)}, bf16[16,8,1536]{2,1,0:T(8,128)(2,1)}, u32[]{:S(2)}, u32[]{:S(2)}) collective-permute-start(bf16[16,8,1536]{2,1,0:T(8,128)(2,1)S(1)} %all-to-all-done.1), channel_id=1, source_target_pairs={{0,1},{1,0},{2,3},{3,2},{4,5},{5,4},{6,7},{7,6},{8,9},{9,8},{10,11... | collective-permute-start | bytes 1179656 | tf_op jit(solution)/shard_map/ppermute | solution.py:62
  71.9 0.0 collective-permute-done.5
  71.9 1.0 %constant_dynamic-update-slice_fusion.refs_2_ = bf16[512,640]{1,0:T(8,128)(2,1)S(1)} fusion(bf16[512,640]{1,0:T(8,128)(2,1)S(1)} %constant_dynamic-update-slice_fusion.1, bf16[256,640]{1,0:T(8,128)(2,1)} %collective-permute-done.5), kind=kLoop, calls=%fused_computation.17 | loop fusion | bytes 655360 | tf_op jit(solution)/shard_map/concatenate | solution.py:243
  72.9 2.2 %collective-permute-start.9 = (bf16[512,640]{1,0:T(8,128)(2,1)S(1)}, bf16[512,640]{1,0:T(8,128)(2,1)}, u32[]{:S(2)}, u32[]{:S(2)}) collective-permute-start(bf16[512,640]{1,0:T(8,128)(2,1)S(1)} %constant_dynamic-update-slice_fusion.refs_2_), channel_id=1, source_target_pairs={{0,1},{1,0},{2,3},{3,2},{4,5},{5,4},{6,7},{7,6},{8,9},{9,8},{10,11... | collective-permute-start | bytes 1966088 | tf_op jit(solution)/shard_map/ppermute | solution.py:62
  75.1 0.8 collective-permute-done.6.refs_3_
  75.9 3.7 %collective-permute-start.10 = (bf16[512,640]{1,0:T(8,128)(2,1)S(1)}, bf16[512,640]{1,0:T(8,128)(2,1)}, u32[]{:S(2)}, u32[]{:S(2)}) collective-permute-start(bf16[512,640]{1,0:T(8,128)(2,1)S(1)} %collective-permute-done.6.refs_3_), channel_id=1, source_target_pairs={{0,1},{1,0},{2,3},{3,2},{4,5},{5,4},{6,7},{7,6},{8,9},{9,8},{10,11... | collective-permute-start | bytes 1966088 | tf_op jit(solution)/shard_map/ppermute | solution.py:62
  79.5 0.0 collective-permute-done.4.refs_1_
  79.6 1.9 %collective-permute-start.8 = (bf16[512,640]{1,0:T(8,128)(2,1)S(1)}, bf16[512,640]{1,0:T(8,128)(2,1)}, u32[]{:S(2)}, u32[]{:S(2)}) collective-permute-start(bf16[512,640]{1,0:T(8,128)(2,1)S(1)} %collective-permute-done.4.refs_1_), channel_id=1, source_target_pairs={{0,1},{1,0},{2,3},{3,2},{4,5},{5,4},{6,7},{7,6},{8,9},{9,8},{10,11... | collective-permute-start | bytes 1966088 | tf_op jit(solution)/shard_map/ppermute | solution.py:62
  81.5 0.1 copy.11.bounds_ref
  81.6 0.1 pad_add_fusion.1.place_ref
  81.7 0.0 collective-permute-done
  81.7 0.0 all-gather.3.cloned.1.call-done
  81.7 0.0 copy-start
  81.7 1.5 %copy-done = bf16[16,112,512]{2,1,0:T(8,128)(2,1)S(1)} copy-done((bf16[16,112,512]{2,1,0:T(8,128)(2,1)S(1)}, bf16[16,112,512]{2,1,0:T(8,128)(2,1)}, u32[]{:S(2)}) %copy-start) | copy-done | bytes 1835032
  83.2 1.8 %shard_map.83 = (bf16[512,640]{1,0:T(8,128)(2,1)S(1)}, bf16[512,256]{1,0:T(8,128)(2,1)S(1)}) custom-call(s32[2]{0:T(128)S(1)} %pad_add_fusion.1.place_ref, bf16[128,1536]{1,0:T(8,128)(2,1)S(1)} %bitcast.9, bf16[128,1536]{1,0:T(8,128)(2,1)} %bitcast.4.other_ref, bf16[8,2,112,512]{3,2,1,0:T(8,128)(2,1)S(1)} %bitcast.10), custom_call_target="tpu_custom_call" | custom-call | flops 5000000000 | tf_op jit(solution)/shard_map/pallas_call | solution.py:110
  85.0 0.0 collective-permute-done.7.refs_4_
  85.1 0.0 collective-permute-done.9.refs_6_
  85.1 0.0 collective-permute-done.10.refs_7_
  85.1 0.0 collective-permute-done.8.refs_5_
  85.1 9.4 %shard_map.84 = bf16[256,256]{1,0:T(8,128)(2,1)} custom-call(bf16[512,640]{1,0:T(8,128)(2,1)S(1)} %get-tuple-element.15.q_ref, bf16[512,256]{1,0:T(8,128)(2,1)S(1)} %get-tuple-element.16.vu_ref, s32[2,4096]{1,0:T(2,128)S(1)} %get-tuple-element.20.low_ref, s32[2,4096]{1,0:T(2,128)S(1)} %get-tuple-element.19.high_ref, s32[256,2]{1,0:T(8,128)S(1)} %copy.11.bounds_ref, ...), custom_call_target="tpu_custom_call" | custom-call | flops 4563402752 | bytes 5242880 | tf_op jit(solution)/shard_map/pallas_call | solution.py:192
  (9 shorter events, 0.1 us)
Async XLA Ops:
  6.5 33.8 %copy-start.2 = (s32[2,32]{1,0:T(2,128)S(1)}, s32[2,32]{1,0:T(2,128)}, u32[]{:S(2)}) copy-start(s32[2,32]{1,0:T(2,128)} %param.15) | copy-start | bytes 772
  6.5 38.7 %copy-start.1 = (bf16[8,1536]{1,0:T(8,128)(2,1)S(1)}, bf16[8,1536]{1,0:T(8,128)(2,1)}, u32[]{:S(2)}) copy-start(bf16[8,1536]{1,0:T(8,128)(2,1)} %param.8) | copy-start | bytes 73732
  8.2 30.1 %all-to-all-start = ((bf16[32,8,640]{2,1,0:T(8,128)(2,1)}), bf16[32,8,640]{2,1,0:T(8,128)(2,1)S(1)}, u32[]{:S(2)}, u32[]{:S(2)}) async-start(bf16[32,8,640]{2,1,0:T(8,128)(2,1)} %get-tuple-element.12), calls=%async_computation | async-start | bytes 655360 | tf_op jit(solution)/shard_map/all_to_all | solution.py:229
  24.7 57.0 %all-gather.3.cloned.1.call-start = ((), (), s32[]{:S(2)}) async-start(), calls=%async_computation.2 | async-start | bytes 2064384 | tf_op jit(solution)/shard_map/all_gather | solution.py:230
  24.8 6.0 %collective-permute-start.1 = (bf16[112,512]{1,0:T(8,128)(2,1)}, bf16[112,512]{1,0:T(8,128)(2,1)S(1)}, u32[]{:S(2)}, u32[]{:S(2)}) collective-permute-start(bf16[112,512]{1,0:T(8,128)(2,1)} %get-tuple-element.14), channel_id=1, source_target_pairs={{0,256},{256,0},{1,257},{257,1},{2,258},{258,2},{3,259},{259,3},{4... | collective-permute-start | bytes 344072 | tf_op jit(solution)/shard_map/ppermute | solution.py:62
  38.3 14.3 %collective-permute-start.3 = (bf16[256,640]{1,0:T(8,128)(2,1)S(1)}, bf16[256,640]{1,0:T(8,128)(2,1)S(1)}, u32[]{:S(2)}, u32[]{:S(2)}) collective-permute-start(bf16[256,640]{1,0:T(8,128)(2,1)S(1)} %bitcast.11), channel_id=1, source_target_pairs={{0,4},{4,0},{1,5},{5,1},{2,6},{6,2},{3,7},{7,3},{8,12},{12,8},{9,1... | collective-permute-start | bytes 983048 | tf_op jit(solution)/shard_map/ppermute | solution.py:62
  40.6 22.6 %copy-start.3 = (s32[24]{0:T(128)S(1)}, s32[24]{0:T(128)}, u32[]{:S(2)}) copy-start(s32[24]{0:T(128)} %param.14) | copy-start | bytes 292
  40.6 19.4 %collective-permute-start.2 = (bf16[256,640]{1,0:T(8,128)(2,1)S(1)}, bf16[256,640]{1,0:T(8,128)(2,1)S(1)}, u32[]{:S(2)}, u32[]{:S(2)}) collective-permute-start(bf16[256,640]{1,0:T(8,128)(2,1)S(1)} %bitcast.12), channel_id=1, source_target_pairs={{0,2},{2,0},{1,3},{3,1},{4,6},{6,4},{5,7},{7,5},{8,10},{10,8},{9,1... | collective-permute-start | bytes 983048 | tf_op jit(solution)/shard_map/ppermute | solution.py:62
  46.0 21.9 %all-to-all-start.1 = ((bf16[16,8,1536]{2,1,0:T(8,128)(2,1)}), bf16[16,8,1536]{2,1,0:T(8,128)(2,1)S(1)}, u32[]{:S(2)}, u32[]{:S(2)}) async-start(bf16[16,8,1536]{2,1,0:T(8,128)(2,1)} %broadcast_in_dim.66), calls=%async_computation.1 | async-start | bytes 786432 | tf_op jit(solution)/shard_map/all_to_all | solution.py:72
  52.7 23.2 %collective-permute-start.6 = (bf16[512,640]{1,0:T(8,128)(2,1)S(1)}, bf16[512,640]{1,0:T(8,128)(2,1)S(1)}, u32[]{:S(2)}, u32[]{:S(2)}) collective-permute-start(bf16[512,640]{1,0:T(8,128)(2,1)S(1)} %pad_maximum_fusion.refs_0_), channel_id=1, source_target_pairs={{0,258},{258,0},{2,256},{256,2},{1,259},{259,1},{3,257},{257,3},{4... | collective-permute-start | bytes 1966088 | tf_op jit(solution)/shard_map/ppermute | solution.py:240
  58.0 21.5 %collective-permute-start.4 = (bf16[512,640]{1,0:T(8,128)(2,1)S(1)}, bf16[512,640]{1,0:T(8,128)(2,1)S(1)}, u32[]{:S(2)}, u32[]{:S(2)}) collective-permute-start(bf16[512,640]{1,0:T(8,128)(2,1)S(1)} %pad_maximum_fusion.refs_0_), channel_id=1, source_target_pairs={{0,256},{256,0},{1,257},{257,1},{2,258},{258,2},{3,259},{259,3},{4... | collective-permute-start | bytes 1966088 | tf_op jit(solution)/shard_map/ppermute | solution.py:62
  60.0 11.8 %collective-permute-start.5 = (bf16[256,640]{1,0:T(8,128)(2,1)S(1)}, bf16[256,640]{1,0:T(8,128)(2,1)}, u32[]{:S(2)}, u32[]{:S(2)}) collective-permute-start(bf16[256,640]{1,0:T(8,128)(2,1)S(1)} %collective-permute-done.2), channel_id=1, source_target_pairs={{0,4},{4,0},{1,5},{5,1},{2,6},{6,2},{3,7},{7,3},{8,12},{12,8},{9,1... | collective-permute-start | bytes 983048 | tf_op jit(solution)/shard_map/ppermute | solution.py:62
  63.2 21.8 %collective-permute-start.7 = (bf16[512,640]{1,0:T(8,128)(2,1)S(1)}, bf16[512,640]{1,0:T(8,128)(2,1)}, u32[]{:S(2)}, u32[]{:S(2)}) collective-permute-start(bf16[512,640]{1,0:T(8,128)(2,1)S(1)} %pad_maximum_fusion.refs_0_), channel_id=1, source_target_pairs={{0,1},{1,0},{2,3},{3,2},{4,5},{5,4},{6,7},{7,6},{8,9},{9,8},{10,11... | collective-permute-start | bytes 1966088 | tf_op jit(solution)/shard_map/ppermute | solution.py:62
  67.9 13.8 %collective-permute-start = (bf16[16,8,1536]{2,1,0:T(8,128)(2,1)S(1)}, bf16[16,8,1536]{2,1,0:T(8,128)(2,1)}, u32[]{:S(2)}, u32[]{:S(2)}) collective-permute-start(bf16[16,8,1536]{2,1,0:T(8,128)(2,1)S(1)} %all-to-all-done.1), channel_id=1, source_target_pairs={{0,1},{1,0},{2,3},{3,2},{4,5},{5,4},{6,7},{7,6},{8,9},{9,8},{10,11... | collective-permute-start | bytes 1179656 | tf_op jit(solution)/shard_map/ppermute | solution.py:62
  72.9 12.2 %collective-permute-start.9 = (bf16[512,640]{1,0:T(8,128)(2,1)S(1)}, bf16[512,640]{1,0:T(8,128)(2,1)}, u32[]{:S(2)}, u32[]{:S(2)}) collective-permute-start(bf16[512,640]{1,0:T(8,128)(2,1)S(1)} %constant_dynamic-update-slice_fusion.refs_2_), channel_id=1, source_target_pairs={{0,1},{1,0},{2,3},{3,2},{4,5},{5,4},{6,7},{7,6},{8,9},{9,8},{10,11... | collective-permute-start | bytes 1966088 | tf_op jit(solution)/shard_map/ppermute | solution.py:62
  75.9 9.2 %collective-permute-start.10 = (bf16[512,640]{1,0:T(8,128)(2,1)S(1)}, bf16[512,640]{1,0:T(8,128)(2,1)}, u32[]{:S(2)}, u32[]{:S(2)}) collective-permute-start(bf16[512,640]{1,0:T(8,128)(2,1)S(1)} %collective-permute-done.6.refs_3_), channel_id=1, source_target_pairs={{0,1},{1,0},{2,3},{3,2},{4,5},{5,4},{6,7},{7,6},{8,9},{9,8},{10,11... | collective-permute-start | bytes 1966088 | tf_op jit(solution)/shard_map/ppermute | solution.py:62
  79.6 5.5 %collective-permute-start.8 = (bf16[512,640]{1,0:T(8,128)(2,1)S(1)}, bf16[512,640]{1,0:T(8,128)(2,1)}, u32[]{:S(2)}, u32[]{:S(2)}) collective-permute-start(bf16[512,640]{1,0:T(8,128)(2,1)S(1)} %collective-permute-done.4.refs_1_), channel_id=1, source_target_pairs={{0,1},{1,0},{2,3},{3,2},{4,5},{5,4},{6,7},{7,6},{8,9},{9,8},{10,11... | collective-permute-start | bytes 1966088 | tf_op jit(solution)/shard_map/ppermute | solution.py:62
  81.7 1.5 %copy-start = (bf16[16,112,512]{2,1,0:T(8,128)(2,1)S(1)}, bf16[16,112,512]{2,1,0:T(8,128)(2,1)}, u32[]{:S(2)}) copy-start(bf16[16,112,512]{2,1,0:T(8,128)(2,1)} %all-gather.3.cloned.1.call-done) | copy-start | bytes 5505028
Sparse Core Ops, SparseCore 0:
  32.6 42.0 all-gather.2

commit v5 on v4

--- a/solution.py
+++ b/solution.py
@@ -225,12 +225,14 @@
 
     kv, packed = lax.optimization_barrier((kv, packed))
     w_pair = jnp.stack([packed, swap(packed, "xl")], axis=0)
+    _, q_latent = lax.optimization_barrier((w_pair, q_latent))
+    q_pair = in_order(xh, q_latent[None], swap(q_latent, "xh")[None], 0)
 
     near = lax.all_to_all(kv, (*Z, "y2"), 0, 0).reshape(256, WIDTH)
     weights = lax.all_gather(w_pair, Z)
 
-    q_latent, _ = lax.optimization_barrier((q_latent, near))
-    q_half = gather_direct(q_latent, ("y2", "y1", "xh"), 16)
+    q_pair, _ = lax.optimization_barrier((q_pair, near))
+    q_half = gather_direct(q_pair, ("y2", "y1"), 8)
     q_core = swap(q_half, "c")
 
     next_y = swap(near, "y1")
@@ -241,6 +243,8 @@
     x2_far, pair = lax.optimization_barrier((x2_near, pair))
     x2_next = swap(x2_far, "y1")
     x2_pair = jnp.concatenate([x2_near, x2_next], axis=0)
+
+    query, value_up = project(jnp.stack([core, xl]), q_half.reshape(128, 1536), q_core.reshape(128, 1536), weights)
 
     mine = [pair, x1_pair, x2_pair, x3_pair]
     theirs = [swap(piece, "c") for piece in mine]
@@ -265,8 +269,6 @@
     q_pos = (xl * 8 + 2 * z2 + z1) * 256 + lax.broadcasted_iota(jnp.int32, (256, 1), 0)
     q_first = jnp.max(jnp.where(doc_starts[None, :] <= q_pos, doc_starts[None, :], 0), axis=1, keepdims=True)
     bounds = jnp.concatenate([q_pos, q_first], axis=1)
-    place = jnp.stack([core, xl])
-    query, value_up = project(place, q_half.reshape(128, 1536), q_core.reshape(128, 1536), weights)
     return attention(query, value_up, mine + theirs, low, high, bounds)
 
 

time: 102 us -> 99.1 us (0.972)
  waiting for transfers between devices: 9.19 us -> 4.3 us
  starting transfers between devices: 59.5 us -> 62.2 us
    ppermute x10 -> x11, starting transfers between devices: 31 us -> 36.3 us  [swap(): return lax.ppermute(x, axis, [(0, 1), (1, 0)])]
    all_to_all x1, waiting for transfers between devices: 5.5 us -> 1.78 us  [body(): near = lax.all_to_all(kv, (*Z, 'y2'), 0, 0).reshape(256, WIDTH)]
    ppermute x1, starting transfers between devices: 5.35 us -> 2.77 us  [body(): x3_pair = lax.ppermute(pair, ('xl', 'xh'), [(0, 3), (3, 0), (1, 2), (2, 1)])]
    ppermute x10 -> x11, waiting for transfers between devices: 2.89 us -> 2.5 us  [swap(): return lax.ppermute(x, axis, [(0, 1), (1, 0)])]
  transfers between devices with their start and end apart: 14 -> 15, of which waited for: 3 -> 2; matrix products, arithmetic and copies ran while one was open for 4% -> 4% of each run, Pallas kernels for 2% -> 2%
where the time goes in v5:
time: 99.1 us; the launch traced here: 98.4 us
  starting transfers between devices  62.2 us (63%)
  between operations  13.8 us (14%)
  Pallas kernels  12.9 us (13%)
  waiting for transfers between devices  4.3 us (4%)
  local copies, waits for them, and re-layouts  3.72 us (4%)
  other arithmetic  1.49 us (2%)
    ppermute x11, starting transfers between devices, swap(): return lax.ppermute(x, axis, [(0, 1), (1, 0)])  36.3 us
    all_to_all x1, starting transfers between devices, body(): near = lax.all_to_all(kv, (*Z, 'y2'), 0, 0).reshape(256, WIDTH)  16.6 us
    pallas_call x1, Pallas kernels, attention(): pl.pallas_call(attention_kernel, out_shape=jax.ShapeDtypeStruct((tokens,...  9.44 us
    all_to_all x1, starting transfers between devices, gather_direct(): lax.all_to_all(jnp.broadcast_to(x[None], (members,) + x.shape), axes, 0, 0)  6.43 us
    ppermute x1, starting transfers between devices, body(): x3_pair = lax.ppermute(pair, ('xl', 'xh'), [(0, 3), (3, 0), (1, 2), (2, 1)])  2.77 us
    ppermute x11, waiting for transfers between devices, swap(): return lax.ppermute(x, axis, [(0, 1), (1, 0)])  2.5 us
  transfers between devices with their start and end apart: 15, of which 2 were waited for; matrix products, arithmetic and copies ran while one was open for 4% of the time, Pallas kernels for 2%

profile of v5, /device:TPU:1, one launch (start us, length us, event | category | flops | bytes accessed | tf_op | source)
XLA Modules:
  0.0 98.4 jit_solution(16796803765156074975)
XLA Ops:
  6.5 0.0 copy-start.2
  6.5 0.0 copy-start.3
  6.5 1.7 %shard_map.82 = (bf16[32,8,640]{2,1,0:T(8,128)(2,1)}, bf16[112,512]{1,0:T(8,128)(2,1)}) custom-call(bf16[8,576]{1,0:T(8,128)(2,1)} %kv_ref.1, bf16[96,256]{1,0:T(8,128)(2,1)} %wp_ref.1, bf16[96,128]{1,0:T(8,128)(2,1)} %wr_ref.1, bf16[32,256]{1,0:T(8,128)(2,1)} %ku_ref.1, bf16[32,256]{1,0:T(8,128)(2,1)} %vu_ref.1), custom_call_target="tpu_custom_call" | custom-call | tf_op jit(solution)/shard_map/pallas_call | solution.py:50
  8.2 0.0 copy-start.1
  8.2 16.6 %all-to-all-start = ((bf16[32,8,640]{2,1,0:T(8,128)(2,1)}), bf16[32,8,640]{2,1,0:T(8,128)(2,1)S(1)}, u32[]{:S(2)}, u32[]{:S(2)}) async-start(bf16[32,8,640]{2,1,0:T(8,128)(2,1)} %get-tuple-element.15), calls=%async_computation | async-start | bytes 655360 | tf_op jit(solution)/shard_map/all_to_all | solution.py:231
  24.8 0.0 all-gather.3.cloned.1.call-start
  24.9 3.1 %collective-permute-start = (bf16[112,512]{1,0:T(8,128)(2,1)}, bf16[112,512]{1,0:T(8,128)(2,1)S(1)}, u32[]{:S(2)}, u32[]{:S(2)}) collective-permute-start(bf16[112,512]{1,0:T(8,128)(2,1)} %get-tuple-element.13), channel_id=1, source_target_pairs={{0,256},{256,0},{1,257},{257,1},{2,258},{258,2},{3,259},{259,3},{4... | collective-permute-start | bytes 344072 | tf_op jit(solution)/shard_map/ppermute | solution.py:62
  28.1 0.1 add_add_fusion
  28.2 0.2 reshape.339
  28.5 2.5 %collective-permute-done = bf16[112,512]{1,0:T(8,128)(2,1)S(1)} collective-permute-done((bf16[112,512]{1,0:T(8,128)(2,1)}, bf16[112,512]{1,0:T(8,128)(2,1)S(1)}, u32[]{:S(2)}, u32[]{:S(2)}) %collective-permute-start) | collective-permute-done | bytes 114720 | tf_op jit(solution)/shard_map/ppermute | solution.py:62
  30.9 0.0 copy-done.1
  30.9 0.7 pad_maximum_fusion.1
  31.7 0.0 all-gather.3.cloned.1.call-update
  31.7 0.1 iota_compare_fusion
  31.8 0.0 copy-done.2
  31.8 4.7 %collective-permute-start.1 = (bf16[8,1536]{1,0:T(8,128)(2,1)S(1)}, bf16[8,1536]{1,0:T(8,128)(2,1)S(1)}, u32[]{:S(2)}, u32[]{:S(2)}) collective-permute-start(bf16[8,1536]{1,0:T(8,128)(2,1)S(1)} %copy-done.2), channel_id=1, source_target_pairs={{0,2},{2,0},{1,3},{3,1},{4,6},{6,4},{5,7},{7,5},{8,10},{10,8},{9,1... | collective-permute-start | bytes 73736 | tf_op jit(solution)/shard_map/ppermute | solution.py:62
  36.4 0.0 copy-done.3
  36.5 0.2 select_reduce_fusion
  36.7 1.8 %all-to-all-done = bf16[32,8,640]{2,1,0:T(8,128)(2,1)S(1)} async-done(((bf16[32,8,640]{2,1,0:T(8,128)(2,1)}), bf16[32,8,640]{2,1,0:T(8,128)(2,1)S(1)}, u32[]{:S(2)}, u32[]{:S(2)}) %all-to-all-start) | async-done | bytes 327712 | tf_op jit(solution)/shard_map/all_to_all | solution.py:231
  38.5 1.9 %collective-permute-start.4 = (bf16[256,640]{1,0:T(8,128)(2,1)S(1)}, bf16[256,640]{1,0:T(8,128)(2,1)S(1)}, u32[]{:S(2)}, u32[]{:S(2)}) collective-permute-start(bf16[256,640]{1,0:T(8,128)(2,1)S(1)} %bitcast.15), channel_id=1, source_target_pairs={{0,4},{4,0},{1,5},{5,1},{2,6},{6,2},{3,7},{7,3},{8,12},{12,8},{9,1... | collective-permute-start | bytes 983048 | tf_op jit(solution)/shard_map/ppermute | solution.py:62
  40.4 0.0 collective-permute-done.1
  40.4 0.0 copy-start.4
  40.4 4.7 %collective-permute-start.3 = (bf16[256,640]{1,0:T(8,128)(2,1)S(1)}, bf16[256,640]{1,0:T(8,128)(2,1)S(1)}, u32[]{:S(2)}, u32[]{:S(2)}) collective-permute-start(bf16[256,640]{1,0:T(8,128)(2,1)S(1)} %bitcast.16), channel_id=1, source_target_pairs={{0,2},{2,0},{1,3},{3,1},{4,6},{6,4},{5,7},{7,5},{8,10},{10,8},{9,1... | collective-permute-start | bytes 983048 | tf_op jit(solution)/shard_map/ppermute | solution.py:62
  45.1 0.8 broadcast_in_dim.68
  45.9 6.4 %all-to-all-start.1 = ((bf16[8,2,8,1536]{3,2,1,0:T(8,128)(2,1)}), bf16[8,2,8,1536]{3,2,1,0:T(8,128)(2,1)S(1)}, u32[]{:S(2)}, u32[]{:S(2)}) async-start(bf16[8,2,8,1536]{3,2,1,0:T(8,128)(2,1)} %broadcast_in_dim.68), calls=%async_computation.1 | async-start | bytes 786432 | tf_op jit(solution)/shard_map/all_to_all | solution.py:72
  52.3 0.0 collective-permute-done.4
  52.3 0.1 pad_maximum_fusion.refs_0_
  52.4 2.8 %collective-permute-start.7 = (bf16[512,640]{1,0:T(8,128)(2,1)S(1)}, bf16[512,640]{1,0:T(8,128)(2,1)S(1)}, u32[]{:S(2)}, u32[]{:S(2)}) collective-permute-start(bf16[512,640]{1,0:T(8,128)(2,1)S(1)} %pad_maximum_fusion.refs_0_), channel_id=1, source_target_pairs={{0,258},{258,0},{2,256},{256,2},{1,259},{259,1},{3,257},{257,3},{4... | collective-permute-start | bytes 1966088 | tf_op jit(solution)/shard_map/ppermute | solution.py:242
  55.1 1.9 %collective-permute-start.5 = (bf16[512,640]{1,0:T(8,128)(2,1)S(1)}, bf16[512,640]{1,0:T(8,128)(2,1)S(1)}, u32[]{:S(2)}, u32[]{:S(2)}) collective-permute-start(bf16[512,640]{1,0:T(8,128)(2,1)S(1)} %pad_maximum_fusion.refs_0_), channel_id=1, source_target_pairs={{0,256},{256,0},{1,257},{257,1},{2,258},{258,2},{3,259},{259,3},{4... | collective-permute-start | bytes 1966088 | tf_op jit(solution)/shard_map/ppermute | solution.py:62
  57.1 0.0 collective-permute-done.3
  57.2 3.4 %collective-permute-start.6 = (bf16[256,640]{1,0:T(8,128)(2,1)S(1)}, bf16[256,640]{1,0:T(8,128)(2,1)}, u32[]{:S(2)}, u32[]{:S(2)}) collective-permute-start(bf16[256,640]{1,0:T(8,128)(2,1)S(1)} %collective-permute-done.3), channel_id=1, source_target_pairs={{0,4},{4,0},{1,5},{5,1},{2,6},{6,2},{3,7},{7,3},{8,12},{12,8},{9,1... | collective-permute-start | bytes 983048 | tf_op jit(solution)/shard_map/ppermute | solution.py:62
  60.5 0.0 copy-done.4
  60.5 0.1 select_reduce_fusion.1
  60.6 4.6 %collective-permute-start.8 = (bf16[512,640]{1,0:T(8,128)(2,1)S(1)}, bf16[512,640]{1,0:T(8,128)(2,1)}, u32[]{:S(2)}, u32[]{:S(2)}) collective-permute-start(bf16[512,640]{1,0:T(8,128)(2,1)S(1)} %pad_maximum_fusion.refs_0_), channel_id=1, source_target_pairs={{0,1},{1,0},{2,3},{3,2},{4,5},{5,4},{6,7},{7,6},{8,9},{9,8},{10,11... | collective-permute-start | bytes 1966088 | tf_op jit(solution)/shard_map/ppermute | solution.py:62
  65.3 0.0 all-to-all-done.1
  65.3 5.2 %collective-permute-start.2 = (bf16[8,2,8,1536]{3,2,1,0:T(8,128)(2,1)S(1)}, bf16[8,2,8,1536]{3,2,1,0:T(8,128)(2,1)}, u32[]{:S(2)}, u32[]{:S(2)}) collective-permute-start(bf16[8,2,8,1536]{3,2,1,0:T(8,128)(2,1)S(1)} %all-to-all-done.1), channel_id=1, source_target_pairs={{0,1},{1,0},{2,3},{3,2},{4,5},{5,4},{6,7},{7,6},{8,9},{9,8},{10,11... | collective-permute-start | bytes 1179656 | tf_op jit(solution)/shard_map/ppermute | solution.py:62
  70.6 0.0 collective-permute-done.6
  70.6 1.0 %constant_dynamic-update-slice_fusion.refs_2_ = bf16[512,640]{1,0:T(8,128)(2,1)S(1)} fusion(bf16[512,640]{1,0:T(8,128)(2,1)S(1)} %constant_dynamic-update-slice_fusion.1, bf16[256,640]{1,0:T(8,128)(2,1)} %collective-permute-done.6), kind=kLoop, calls=%fused_computation.20 | loop fusion | bytes 655360 | tf_op jit(solution)/shard_map/concatenate | solution.py:245
  71.6 2.5 %collective-permute-start.10 = (bf16[512,640]{1,0:T(8,128)(2,1)S(1)}, bf16[512,640]{1,0:T(8,128)(2,1)}, u32[]{:S(2)}, u32[]{:S(2)}) collective-permute-start(bf16[512,640]{1,0:T(8,128)(2,1)S(1)} %constant_dynamic-update-slice_fusion.refs_2_), channel_id=1, source_target_pairs={{0,1},{1,0},{2,3},{3,2},{4,5},{5,4},{6,7},{7,6},{8,9},{9,8},{10,11... | collective-permute-start | bytes 1966088 | tf_op jit(solution)/shard_map/ppermute | solution.py:62
  74.1 0.0 collective-permute-done.7.refs_3_
  74.1 1.9 %collective-permute-start.11 = (bf16[512,640]{1,0:T(8,128)(2,1)S(1)}, bf16[512,640]{1,0:T(8,128)(2,1)}, u32[]{:S(2)}, u32[]{:S(2)}) collective-permute-start(bf16[512,640]{1,0:T(8,128)(2,1)S(1)} %collective-permute-done.7.refs_3_), channel_id=1, source_target_pairs={{0,1},{1,0},{2,3},{3,2},{4,5},{5,4},{6,7},{7,6},{8,9},{9,8},{10,11... | collective-permute-start | bytes 1966088 | tf_op jit(solution)/shard_map/ppermute | solution.py:62
  76.0 0.0 collective-permute-done.5.refs_1_
  76.0 2.4 %collective-permute-start.9 = (bf16[512,640]{1,0:T(8,128)(2,1)S(1)}, bf16[512,640]{1,0:T(8,128)(2,1)}, u32[]{:S(2)}, u32[]{:S(2)}) collective-permute-start(bf16[512,640]{1,0:T(8,128)(2,1)S(1)} %collective-permute-done.5.refs_1_), channel_id=1, source_target_pairs={{0,1},{1,0},{2,3},{3,2},{4,5},{5,4},{6,7},{7,6},{8,9},{9,8},{10,11... | collective-permute-start | bytes 1966088 | tf_op jit(solution)/shard_map/ppermute | solution.py:62
  78.5 0.1 copy.11.bounds_ref
  78.6 0.1 pad_add_fusion.1.place_ref
  78.7 0.0 collective-permute-done.2
  78.7 0.0 all-gather.3.cloned.1.call-done
  78.7 0.0 copy-start
  78.7 1.5 %copy-done = bf16[16,112,512]{2,1,0:T(8,128)(2,1)S(1)} copy-done((bf16[16,112,512]{2,1,0:T(8,128)(2,1)S(1)}, bf16[16,112,512]{2,1,0:T(8,128)(2,1)}, u32[]{:S(2)}) %copy-start) | copy-done | bytes 1835032
  80.2 1.8 %shard_map.83 = (bf16[512,640]{1,0:T(8,128)(2,1)S(1)}, bf16[512,256]{1,0:T(8,128)(2,1)S(1)}) custom-call(s32[2]{0:T(128)S(1)} %pad_add_fusion.1.place_ref, bf16[128,1536]{1,0:T(8,128)(2,1)S(1)} %bitcast.13, bf16[128,1536]{1,0:T(8,128)(2,1)} %bitcast.8.other_ref, bf16[8,2,112,512]{3,2,1,0:T(8,128)(2,1)S(1)} %bitcast.14), custom_call_target="tpu_custom_call" | custom-call | flops 5000000000 | tf_op jit(solution)/shard_map/pallas_call | solution.py:110
  82.0 0.0 collective-permute-done.8.refs_4_
  82.0 0.0 collective-permute-done.10.refs_6_
  82.1 0.0 collective-permute-done.11.refs_7_
  82.1 0.0 collective-permute-done.9.refs_5_
  82.1 9.4 %shard_map.84 = bf16[256,256]{1,0:T(8,128)(2,1)} custom-call(bf16[512,640]{1,0:T(8,128)(2,1)S(1)} %get-tuple-element.17.q_ref, bf16[512,256]{1,0:T(8,128)(2,1)S(1)} %get-tuple-element.18.vu_ref, s32[2,4096]{1,0:T(2,128)S(1)} %get-tuple-element.22.low_ref, s32[2,4096]{1,0:T(2,128)S(1)} %get-tuple-element.21.high_ref, s32[256,2]{1,0:T(8,128)S(1)} %copy.11.bounds_ref, ...), custom_call_target="tpu_custom_call" | custom-call | flops 4563402752 | bytes 5242880 | tf_op jit(solution)/shard_map/pallas_call | solution.py:192
  (11 shorter events, 0.1 us)
Async XLA Ops:
  6.5 25.2 %copy-start.2 = (bf16[8,1536]{1,0:T(8,128)(2,1)S(1)}, bf16[8,1536]{1,0:T(8,128)(2,1)}, u32[]{:S(2)}) copy-start(bf16[8,1536]{1,0:T(8,128)(2,1)} %param.8) | copy-start | bytes 73732
  6.5 29.9 %copy-start.3 = (s32[2,32]{1,0:T(2,128)S(1)}, s32[2,32]{1,0:T(2,128)}, u32[]{:S(2)}) copy-start(s32[2,32]{1,0:T(2,128)} %param.15) | copy-start | bytes 772
  8.2 22.8 %copy-start.1 = (bf16[112,512]{1,0:T(8,128)(2,1)S(1)}, bf16[112,512]{1,0:T(8,128)(2,1)}, u32[]{:S(2)}) copy-start(bf16[112,512]{1,0:T(8,128)(2,1)} %get-tuple-element.13) | copy-start | bytes 344068
  8.2 30.3 %all-to-all-start = ((bf16[32,8,640]{2,1,0:T(8,128)(2,1)}), bf16[32,8,640]{2,1,0:T(8,128)(2,1)S(1)}, u32[]{:S(2)}, u32[]{:S(2)}) async-start(bf16[32,8,640]{2,1,0:T(8,128)(2,1)} %get-tuple-element.15), calls=%async_computation | async-start | bytes 655360 | tf_op jit(solution)/shard_map/all_to_all | solution.py:231
  24.8 53.9 %all-gather.3.cloned.1.call-start = ((), (), s32[]{:S(2)}) async-start(), calls=%async_computation.2 | async-start | bytes 2064384 | tf_op jit(solution)/shard_map/all_gather | solution.py:232
  24.9 6.0 %collective-permute-start = (bf16[112,512]{1,0:T(8,128)(2,1)}, bf16[112,512]{1,0:T(8,128)(2,1)S(1)}, u32[]{:S(2)}, u32[]{:S(2)}) collective-permute-start(bf16[112,512]{1,0:T(8,128)(2,1)} %get-tuple-element.13), channel_id=1, source_target_pairs={{0,256},{256,0},{1,257},{257,1},{2,258},{258,2},{3,259},{259,3},{4... | collective-permute-start | bytes 344072 | tf_op jit(solution)/shard_map/ppermute | solution.py:62
  31.8 8.6 %collective-permute-start.1 = (bf16[8,1536]{1,0:T(8,128)(2,1)S(1)}, bf16[8,1536]{1,0:T(8,128)(2,1)S(1)}, u32[]{:S(2)}, u32[]{:S(2)}) collective-permute-start(bf16[8,1536]{1,0:T(8,128)(2,1)S(1)} %copy-done.2), channel_id=1, source_target_pairs={{0,2},{2,0},{1,3},{3,1},{4,6},{6,4},{5,7},{7,5},{8,10},{10,8},{9,1... | collective-permute-start | bytes 73736 | tf_op jit(solution)/shard_map/ppermute | solution.py:62
  38.5 13.8 %collective-permute-start.4 = (bf16[256,640]{1,0:T(8,128)(2,1)S(1)}, bf16[256,640]{1,0:T(8,128)(2,1)S(1)}, u32[]{:S(2)}, u32[]{:S(2)}) collective-permute-start(bf16[256,640]{1,0:T(8,128)(2,1)S(1)} %bitcast.15), channel_id=1, source_target_pairs={{0,4},{4,0},{1,5},{5,1},{2,6},{6,2},{3,7},{7,3},{8,12},{12,8},{9,1... | collective-permute-start | bytes 983048 | tf_op jit(solution)/shard_map/ppermute | solution.py:62
  40.4 20.1 %copy-start.4 = (s32[24]{0:T(128)S(1)}, s32[24]{0:T(128)}, u32[]{:S(2)}) copy-start(s32[24]{0:T(128)} %param.14) | copy-start | bytes 292
  40.4 16.7 %collective-permute-start.3 = (bf16[256,640]{1,0:T(8,128)(2,1)S(1)}, bf16[256,640]{1,0:T(8,128)(2,1)S(1)}, u32[]{:S(2)}, u32[]{:S(2)}) collective-permute-start(bf16[256,640]{1,0:T(8,128)(2,1)S(1)} %bitcast.16), channel_id=1, source_target_pairs={{0,2},{2,0},{1,3},{3,1},{4,6},{6,4},{5,7},{7,5},{8,10},{10,8},{9,1... | collective-permute-start | bytes 983048 | tf_op jit(solution)/shard_map/ppermute | solution.py:62
  45.9 19.4 %all-to-all-start.1 = ((bf16[8,2,8,1536]{3,2,1,0:T(8,128)(2,1)}), bf16[8,2,8,1536]{3,2,1,0:T(8,128)(2,1)S(1)}, u32[]{:S(2)}, u32[]{:S(2)}) async-start(bf16[8,2,8,1536]{3,2,1,0:T(8,128)(2,1)} %broadcast_in_dim.68), calls=%async_computation.1 | async-start | bytes 786432 | tf_op jit(solution)/shard_map/all_to_all | solution.py:72
  52.4 21.7 %collective-permute-start.7 = (bf16[512,640]{1,0:T(8,128)(2,1)S(1)}, bf16[512,640]{1,0:T(8,128)(2,1)S(1)}, u32[]{:S(2)}, u32[]{:S(2)}) collective-permute-start(bf16[512,640]{1,0:T(8,128)(2,1)S(1)} %pad_maximum_fusion.refs_0_), channel_id=1, source_target_pairs={{0,258},{258,0},{2,256},{256,2},{1,259},{259,1},{3,257},{257,3},{4... | collective-permute-start | bytes 1966088 | tf_op jit(solution)/shard_map/ppermute | solution.py:242
  55.1 20.9 %collective-permute-start.5 = (bf16[512,640]{1,0:T(8,128)(2,1)S(1)}, bf16[512,640]{1,0:T(8,128)(2,1)S(1)}, u32[]{:S(2)}, u32[]{:S(2)}) collective-permute-start(bf16[512,640]{1,0:T(8,128)(2,1)S(1)} %pad_maximum_fusion.refs_0_), channel_id=1, source_target_pairs={{0,256},{256,0},{1,257},{257,1},{2,258},{258,2},{3,259},{259,3},{4... | collective-permute-start | bytes 1966088 | tf_op jit(solution)/shard_map/ppermute | solution.py:62
  57.2 13.4 %collective-permute-start.6 = (bf16[256,640]{1,0:T(8,128)(2,1)S(1)}, bf16[256,640]{1,0:T(8,128)(2,1)}, u32[]{:S(2)}, u32[]{:S(2)}) collective-permute-start(bf16[256,640]{1,0:T(8,128)(2,1)S(1)} %collective-permute-done.3), channel_id=1, source_target_pairs={{0,4},{4,0},{1,5},{5,1},{2,6},{6,2},{3,7},{7,3},{8,12},{12,8},{9,1... | collective-permute-start | bytes 983048 | tf_op jit(solution)/shard_map/ppermute | solution.py:62
  60.6 21.4 %collective-permute-start.8 = (bf16[512,640]{1,0:T(8,128)(2,1)S(1)}, bf16[512,640]{1,0:T(8,128)(2,1)}, u32[]{:S(2)}, u32[]{:S(2)}) collective-permute-start(bf16[512,640]{1,0:T(8,128)(2,1)S(1)} %pad_maximum_fusion.refs_0_), channel_id=1, source_target_pairs={{0,1},{1,0},{2,3},{3,2},{4,5},{5,4},{6,7},{7,6},{8,9},{9,8},{10,11... | collective-permute-start | bytes 1966088 | tf_op jit(solution)/shard_map/ppermute | solution.py:62
  65.3 13.4 %collective-permute-start.2 = (bf16[8,2,8,1536]{3,2,1,0:T(8,128)(2,1)S(1)}, bf16[8,2,8,1536]{3,2,1,0:T(8,128)(2,1)}, u32[]{:S(2)}, u32[]{:S(2)}) collective-permute-start(bf16[8,2,8,1536]{3,2,1,0:T(8,128)(2,1)S(1)} %all-to-all-done.1), channel_id=1, source_target_pairs={{0,1},{1,0},{2,3},{3,2},{4,5},{5,4},{6,7},{7,6},{8,9},{9,8},{10,11... | collective-permute-start | bytes 1179656 | tf_op jit(solution)/shard_map/ppermute | solution.py:62
  71.6 10.4 %collective-permute-start.10 = (bf16[512,640]{1,0:T(8,128)(2,1)S(1)}, bf16[512,640]{1,0:T(8,128)(2,1)}, u32[]{:S(2)}, u32[]{:S(2)}) collective-permute-start(bf16[512,640]{1,0:T(8,128)(2,1)S(1)} %constant_dynamic-update-slice_fusion.refs_2_), channel_id=1, source_target_pairs={{0,1},{1,0},{2,3},{3,2},{4,5},{5,4},{6,7},{7,6},{8,9},{9,8},{10,11... | collective-permute-start | bytes 1966088 | tf_op jit(solution)/shard_map/ppermute | solution.py:62
  74.1 7.9 %collective-permute-start.11 = (bf16[512,640]{1,0:T(8,128)(2,1)S(1)}, bf16[512,640]{1,0:T(8,128)(2,1)}, u32[]{:S(2)}, u32[]{:S(2)}) collective-permute-start(bf16[512,640]{1,0:T(8,128)(2,1)S(1)} %collective-permute-done.7.refs_3_), channel_id=1, source_target_pairs={{0,1},{1,0},{2,3},{3,2},{4,5},{5,4},{6,7},{7,6},{8,9},{9,8},{10,11... | collective-permute-start | bytes 1966088 | tf_op jit(solution)/shard_map/ppermute | solution.py:62
  76.0 6.0 %collective-permute-start.9 = (bf16[512,640]{1,0:T(8,128)(2,1)S(1)}, bf16[512,640]{1,0:T(8,128)(2,1)}, u32[]{:S(2)}, u32[]{:S(2)}) collective-permute-start(bf16[512,640]{1,0:T(8,128)(2,1)S(1)} %collective-permute-done.5.refs_1_), channel_id=1, source_target_pairs={{0,1},{1,0},{2,3},{3,2},{4,5},{5,4},{6,7},{7,6},{8,9},{9,8},{10,11... | collective-permute-start | bytes 1966088 | tf_op jit(solution)/shard_map/ppermute | solution.py:62
  78.7 1.5 %copy-start = (bf16[16,112,512]{2,1,0:T(8,128)(2,1)S(1)}, bf16[16,112,512]{2,1,0:T(8,128)(2,1)}, u32[]{:S(2)}) copy-start(bf16[16,112,512]{2,1,0:T(8,128)(2,1)} %all-gather.3.cloned.1.call-done) | copy-start | bytes 5505028
Sparse Core Ops, SparseCore 0:
  31.8 42.0 all-gather.2
